TPU v7x, 32 devices: a whole 2x2x4 slice. The times are simulated.
32 devices in a mesh: blocks: 8 (over z, x), chan: 4 (over y, core).
Axes of the slice: x: 2, y: 2, z: 4, core: 2. Of those that a mesh axis runs over, the one named last changes fastest.
Arguments:
- fine_input: bfloat16 [128, 64, 512], P('blocks', 'chan'), may hold values from -6 to 6
- block_counts: int32 [8], replicated, may hold values from 8 to 16, as said below
- fine_weight: bfloat16 [7, 64, 64], P(None, 'chan'), may hold values from -0.25 to 0.25
- fine_bias: float32 [64], P('chan'), may hold values from -3 to 3
- coarse_weight: bfloat16 [7, 64, 64], P(None, 'chan'), may hold values from -0.25 to 0.25
- coarse_bias: float32 [64], P('chan'), may hold values from -3 to 3
- coarse_cotangent: bfloat16 [16, 64, 512], P('blocks', 'chan'), may hold values from -48 to 48
Outputs:
- coarser_level_output: bfloat16 [16, 64, 512], P('blocks', 'chan')
- fine_grad: bfloat16 [128, 64, 512], P('blocks', 'chan')
- fine_weight_grad: float32 [7, 64, 64], P(None, 'chan')
- fine_bias_grad: float32 [64], P('chan')
- coarse_weight_grad: float32 [7, 64, 64], P(None, 'chan')
- coarse_bias_grad: float32 [64], P('chan')
Inputs may be any that keep to these rules, and one draw needn't show every extreme that they name: `block_counts`: fine blocks held by each device of blocks; they sum to 96, and some device holds exactly 16.
All inputs are finite; a program needn't handle non-finite values.
Results may differ from a plain program's by a relative error of at most 0.017.
Values may be sent and summed in bfloat16 or wider, within the bound.
A program may use at most 64 MiB of HBM per device.

v0:
```python
import jax
import jax.numpy as jnp
from jax import lax
from jax.sharding import PartitionSpec as P

EDGE = 8


TAP_PAIRS = (0, 2, 1, 4, 3, 6, 5)


def from_behind(block, axis, distance):
    devices = range(lax.axis_size(axis))
    route = [(i - distance, i) for i in devices if i - distance in devices]
    return lax.ppermute(block, axis, route)


def block_layers(block_cube):
    channels, edge_cells = (block_cube.shape[0], block_cube.shape[1])
    side_layers = [
        block_cube[:, :, :, 0],
        block_cube[:, :, :, -1],
        block_cube[:, :, 0, :],
        block_cube[:, :, -1, :],
        block_cube[:, 0],
        block_cube[:, -1],
    ]
    return jnp.stack(side_layers).reshape(6, channels, edge_cells * edge_cells)


def block_views(block_cube, halo_layers):
    channels, edge_cells = (block_cube.shape[0], block_cube.shape[1])
    sheets = halo_layers.reshape(6, channels, edge_cells, edge_cells)
    minus_x = jnp.concatenate([sheets[0][:, :, :, None], block_cube[:, :, :, :-1]], axis=3)
    plus_x = jnp.concatenate([block_cube[:, :, :, 1:], sheets[1][:, :, :, None]], axis=3)
    minus_y = jnp.concatenate([sheets[2][:, :, None, :], block_cube[:, :, :-1, :]], axis=2)
    plus_y = jnp.concatenate([block_cube[:, :, 1:, :], sheets[3][:, :, None, :]], axis=2)
    minus_z = jnp.concatenate([sheets[4][:, None], block_cube[:, :-1]], axis=1)
    plus_z = jnp.concatenate([block_cube[:, 1:], sheets[5][:, None]], axis=1)
    stacked = jnp.stack([block_cube, minus_x, plus_x, minus_y, plus_y, minus_z, plus_z])
    return stacked.reshape(7 * channels, edge_cells**3)


def slope_of(pre_values):
    sigmoid_values = jax.nn.sigmoid(pre_values)
    return sigmoid_values * (1.0 + pre_values * (1.0 - sigmoid_values))


def fine_halo(layer_table, block_ids, first_block, live_count, total_blocks):
    slot_count = layer_table.shape[0]
    plus_side = layer_table[:, 1::2]
    minus_side = layer_table[:, 0::2]
    tail_layers = lax.dynamic_slice_in_dim(plus_side, live_count - 4, 4, 0)
    from_lower = from_behind(tail_layers, "blocks", 1)
    from_upper = from_behind(minus_side[:4], "blocks", -1)
    table_minus = jnp.concatenate([from_lower, plus_side], axis=0)
    table_plus = jnp.concatenate([minus_side, from_upper], axis=0)
    strides = jnp.array([1, 2, 4], jnp.int32)
    lower_ids = block_ids[:, None] - strides[None, :]
    upper_octant_index = block_ids[:, None] + strides[None, :]
    end_block = first_block + live_count
    rows_minus = jnp.clip(lower_ids - first_block + 4, 0, slot_count + 3)
    rows_plus = jnp.clip(
        jnp.where(
            upper_octant_index < end_block,
            upper_octant_index - first_block,
            slot_count + upper_octant_index - end_block,
        ),
        0,
        slot_count + 3,
    )
    columns = jnp.arange(3, dtype=jnp.int32)[None, :]
    got_minus = table_minus[rows_minus, columns]
    got_plus = table_plus[rows_plus, columns]
    parity_x = block_ids % 2
    parity_y = block_ids // 2 % 2
    keep_minus = jnp.stack([parity_x == 1, parity_y == 1, block_ids >= 4], axis=1)
    keep_plus = jnp.stack([parity_x == 0, parity_y == 0, block_ids + 4 < total_blocks], axis=1)
    zero_value = jnp.zeros((), layer_table.dtype)
    got_minus = jnp.where(keep_minus[:, :, None, None], got_minus, zero_value)
    got_plus = jnp.where(keep_plus[:, :, None, None], got_plus, zero_value)
    merged = jnp.stack([got_minus, got_plus], axis=2)
    return merged.reshape(layer_table.shape)


def coarse_halo(layer_table, coarse_ids, coarse_first, coarse_count, coarse_total):
    slot_count = layer_table.shape[0]
    top_layers = layer_table[:, 5]
    bottom_layers = layer_table[:, 4]
    last_top = lax.dynamic_index_in_dim(top_layers, coarse_count - 1, 0, keepdims=False)
    from_lower = from_behind(last_top, "blocks", 1)
    from_upper = from_behind(bottom_layers[0], "blocks", -1)
    table_minus = jnp.concatenate([from_lower[None], top_layers], axis=0)
    table_plus = jnp.concatenate([bottom_layers, from_upper[None]], axis=0)
    rows_minus = jnp.clip(coarse_ids - coarse_first, 0, slot_count)
    rows_plus = jnp.clip(
        jnp.where(
            coarse_ids + 1 < coarse_first + coarse_count, coarse_ids + 1 - coarse_first, slot_count
        ),
        0,
        slot_count,
    )
    zero_value = jnp.zeros((), layer_table.dtype)
    below_layer = jnp.where((coarse_ids >= 1)[:, None, None], table_minus[rows_minus], zero_value)
    above_layer = jnp.where(
        (coarse_ids + 1 < coarse_total)[:, None, None], table_plus[rows_plus], zero_value
    )
    flat_zero = jnp.zeros_like(below_layer)
    return jnp.stack([flat_zero, flat_zero, flat_zero, flat_zero, below_layer, above_layer], axis=1)


def apply_blocks(matrix, block_cubes, halo_table):

    def one_block(operands):
        return jnp.dot(
            matrix, block_views(operands[0], operands[1]), preferred_element_type=jnp.float32
        )

    return lax.map(one_block, (block_cubes, halo_table))


def weight_block(operands):
    tap_views = block_views(operands[0], operands[1])
    return lax.dot_general(
        operands[2], tap_views, (((1,), (1,)), ((), ())), preferred_element_type=jnp.float32
    )


def restrict_blocks(hidden, half_edge):
    count, width = (hidden.shape[0], hidden.shape[1])
    shaped = hidden.reshape(count, width, half_edge, 2, half_edge, 2, half_edge, 2)
    return (
        (jnp.sum(shaped, axis=(3, 5, 7), dtype=jnp.float32) * 0.125)
        .astype(jnp.bfloat16)
        .reshape(count, width, half_edge**3)
    )


def local(
    fine_input, block_counts, fine_weight, fine_bias, coarse_weight, coarse_bias, coarse_cotangent
):
    slot_count, group_size, cell_count = fine_input.shape
    coarse_slots = coarse_cotangent.shape[0]
    channels = fine_weight.shape[2]
    half_edge = EDGE // 2
    octant_cells = half_edge**3
    pair_index = jnp.array(TAP_PAIRS, jnp.int32)
    device = lax.axis_index("blocks")
    starts = jnp.cumsum(block_counts) - block_counts
    first_block = starts[device]
    live_count = block_counts[device]
    end_block = first_block + live_count
    total_blocks = jnp.sum(block_counts)
    coarse_total = total_blocks // 8
    coarse_first = (first_block + 7) // 8
    coarse_count = (end_block + 7) // 8 - coarse_first
    block_ids = first_block + jnp.arange(slot_count, dtype=jnp.int32)
    coarse_ids = coarse_first + jnp.arange(coarse_slots, dtype=jnp.int32)
    live_mask = (jnp.arange(slot_count) < live_count)[:, None, None]
    coarse_live = (jnp.arange(coarse_slots) < coarse_count)[:, None, None]
    full_input = lax.all_gather(fine_input, "chan", axis=1, tiled=True)
    fine_cubes = full_input.reshape(slot_count, channels, EDGE, EDGE, EDGE)
    input_halos = fine_halo(
        jax.vmap(block_layers)(fine_cubes), block_ids, first_block, live_count, total_blocks
    )
    forward_fine = fine_weight.transpose(1, 0, 2).reshape(group_size, 7 * channels)
    pre_fine = apply_blocks(forward_fine, fine_cubes, input_halos) + fine_bias[None, :, None]
    octants = restrict_blocks(jax.nn.silu(pre_fine).astype(jnp.bfloat16), half_edge)
    upper_octants = from_behind(octants[:7], "blocks", -1)
    octant_table = jnp.concatenate([octants, upper_octants], axis=0)
    children = coarse_ids[:, None] * 8 + jnp.arange(8, dtype=jnp.int32)[None, :]
    child_rows = jnp.clip(
        jnp.where(children < end_block, children - first_block, slot_count + children - end_block),
        0,
        slot_count + 6,
    )
    gathered = octant_table[child_rows]
    coarse_local = (
        gathered.reshape(coarse_slots, 2, 2, 2, group_size, half_edge, half_edge, half_edge)
        .transpose(0, 4, 1, 5, 2, 6, 3, 7)
        .reshape(coarse_slots, group_size, cell_count)
    )
    coarse_local = jnp.where(coarse_live, coarse_local, jnp.zeros((), jnp.bfloat16))
    coarse_full = lax.all_gather(coarse_local, "chan", axis=1, tiled=True)
    coarse_cubes = coarse_full.reshape(coarse_slots, channels, EDGE, EDGE, EDGE)
    coarse_in_halos = coarse_halo(
        jax.vmap(block_layers)(coarse_cubes), coarse_ids, coarse_first, coarse_count, coarse_total
    )
    coarser_level_views = jax.vmap(block_views)(coarse_cubes, coarse_in_halos)
    forward_coarser_level = coarse_weight.transpose(1, 0, 2).reshape(group_size, 7 * channels)
    pre_coarse = (
        jnp.einsum(
            "ln,enp->elp",
            forward_coarser_level,
            coarser_level_views,
            preferred_element_type=jnp.float32,
        )
        + coarse_bias[None, :, None]
    )
    coarser_level_output = jnp.where(coarse_live, jax.nn.silu(pre_coarse), 0.0).astype(jnp.bfloat16)
    coarser_level_delta = jnp.where(
        coarse_live, coarse_cotangent.astype(jnp.float32) * slope_of(pre_coarse), 0.0
    ).astype(jnp.bfloat16)
    coarse_weight_grad = jnp.einsum(
        "zlc,znc->ln", coarser_level_delta, coarser_level_views, preferred_element_type=jnp.float32
    )
    coarse_weight_grad = coarse_weight_grad.reshape(group_size, 7, channels).transpose(1, 0, 2)
    coarse_bias_grad = jnp.sum(coarser_level_delta, axis=(0, 2), dtype=jnp.float32)
    coarse_weight_grad, coarse_bias_grad = lax.psum(
        (coarse_weight_grad, coarse_bias_grad), "blocks"
    )
    delta_cubes = coarser_level_delta.reshape(coarse_slots, group_size, EDGE, EDGE, EDGE)
    delta_halos = coarse_halo(
        jax.vmap(block_layers)(delta_cubes), coarse_ids, coarse_first, coarse_count, coarse_total
    )
    delta_window_views = jax.vmap(block_views)(delta_cubes, delta_halos)
    backward_coarser_level = (
        coarse_weight[pair_index].transpose(2, 0, 1).reshape(channels, 7 * group_size)
    )
    partial_sums = jnp.einsum(
        "ur,mre->mue",
        backward_coarser_level,
        delta_window_views,
        preferred_element_type=jnp.float32,
    )
    coarse_back = lax.psum_scatter(
        partial_sums.astype(jnp.bfloat16), "chan", scatter_dimension=1, tiled=True
    ).astype(jnp.float32)
    coarse_back = jnp.where(coarse_live, coarse_back, 0.0).astype(jnp.bfloat16)
    coarse_octants = (
        coarse_back.reshape(coarse_slots, group_size, 2, half_edge, 2, half_edge, 2, half_edge)
        .transpose(0, 2, 4, 6, 1, 3, 5, 7)
        .reshape(coarse_slots * 8, group_size, octant_cells)
    )
    last_octants = lax.dynamic_slice_in_dim(coarse_octants, (coarse_count - 1) * 8 + 1, 7, 0)
    lower_octants = from_behind(last_octants, "blocks", 1)
    back_table = jnp.concatenate([coarse_octants, lower_octants], axis=0)
    parents = block_ids // 8
    octant_ids = block_ids % 8
    back_rows = jnp.clip(
        jnp.where(
            parents >= coarse_first,
            (parents - coarse_first) * 8 + octant_ids,
            coarse_slots * 8 + octant_ids - 1,
        ),
        0,
        coarse_slots * 8 + 6,
    )
    picked_rows = back_table[back_rows]
    picked = picked_rows.reshape(slot_count, group_size, half_edge, 1, half_edge, 1, half_edge, 1)
    widened = jnp.broadcast_to(
        picked, (slot_count, group_size, half_edge, 2, half_edge, 2, half_edge, 2)
    ).reshape(slot_count, group_size, cell_count)
    fine_delta = jnp.where(
        live_mask, widened.astype(jnp.float32) * 0.125 * slope_of(pre_fine), 0.0
    ).astype(jnp.bfloat16)
    fine_weight_grad = jnp.sum(lax.map(weight_block, (fine_cubes, input_halos, fine_delta)), axis=0)
    fine_weight_grad = fine_weight_grad.reshape(group_size, 7, channels).transpose(1, 0, 2)
    fine_bias_grad = jnp.sum(fine_delta, axis=(0, 2), dtype=jnp.float32)
    fine_delta_cubes = fine_delta.reshape(slot_count, group_size, EDGE, EDGE, EDGE)
    fine_delta_halos = fine_halo(
        jax.vmap(block_layers)(fine_delta_cubes), block_ids, first_block, live_count, total_blocks
    )
    back_fine = fine_weight[pair_index].transpose(2, 0, 1).reshape(channels, 7 * group_size)
    fine_partial = apply_blocks(back_fine, fine_delta_cubes, fine_delta_halos)
    fine_back = lax.psum_scatter(
        fine_partial.astype(jnp.bfloat16), "chan", scatter_dimension=1, tiled=True
    ).astype(jnp.float32)
    fine_grad = jnp.where(live_mask, fine_back, 0.0).astype(jnp.bfloat16)
    fine_weight_grad, fine_bias_grad = lax.psum((fine_weight_grad, fine_bias_grad), "blocks")
    fine_norm = jnp.sqrt(total_blocks.astype(jnp.float32) * cell_count)
    coarse_norm = jnp.sqrt(coarse_total.astype(jnp.float32) * cell_count)
    return (
        coarser_level_output,
        fine_grad,
        fine_weight_grad / fine_norm,
        fine_bias_grad / fine_norm,
        coarse_weight_grad / coarse_norm,
        coarse_bias_grad / coarse_norm,
    )


def solution(mesh):
    placed = (
        P("blocks", "chan", None),
        P(),
        P(None, "chan", None),
        P("chan"),
        P(None, "chan", None),
        P("chan"),
        P("blocks", "chan", None),
    )
    return jax.shard_map(
        local,
        mesh=mesh,
        in_specs=placed,
        out_specs=(
            P("blocks", "chan", None),
            P("blocks", "chan", None),
            P(None, "chan", None),
            P("chan"),
            P(None, "chan", None),
            P("chan"),
        ),
        check_vma=False,
    )
```

profile of v0, /device:TPU:0, one launch (start us, length us, event | category | flops | bytes accessed | tf_op | source)
XLA Modules:
  0.0 473.7 jit_solution(5004367994010666882)
XLA Ops:
  7.2 1.8 copy.593
  9.1 1.2 dynamic_slice.50
  11.2 1.3 fusion.85
  14.8 1.3 fusion.46
  20.7 1.2 add_compare_fusion.2
  25.8 3.8 all-gather.2.cloned.1.call-done
  29.6 3.1 copy.594
  32.7 3.4 fusion.74
  40.8 4.1 collective-permute-start
  45.9 1.3 collective-permute-start.1
  47.2 1.5 collective-permute-done
  50.8 4.1 collective-permute-done.1
  58.3 65.3 %while.33 = (s32[]{:T(128)}, f32[16,16,512]{2,1,0:T(8,128)}, bf16[16,64,8,8,8]{1,4,3,2,0:T(8,128)(2,1)}, bf16[16,6,64,64]{2,3,1,0:T(8,128)(2,1)S(1)}, bf16[16,448]{1,0:T(8,128)(2,1)S(1)}) while((s32[]{:T(128)}, f32[16,16,512]{2,1,0:T(8,128)}, bf16[16,64,8,8,8]{1,4,3,2,0:T(8,128)(2,1)}, bf16[16,6,64,64]{2,3,1,0:T(8,128)(2,1)S(1)}, ...), condition=%wide.region_3.4_spmd.clone, body=%wide.region_2.3_spmd.sunk.clone | while | flops 8126471 | bytes 5126805 | solution.py:119
  123.6 1.6 fusion.25
  125.2 3.7 copy.605
  128.9 2.8 reduce_sum.46
  131.9 1.3 collective-permute-start.2
  134.2 3.5 collective-permute-done.2
  138.8 5.4 %all_gather.7 = bf16[2,64,512]{2,1,0:T(8,128)(2,1)S(1)} all-gather(bf16[2,16,512]{2,1,0:T(8,128)(2,1)S(1)} %broadcast_select_fusion.4), channel_id=1, replica_groups=mesh['blocks'=8,'chan'=4] {'chan'}, dimensions={1}, use_global_device_ids=true | all-gather | bytes 163840 | tf_op jit(solution)/shard_map/all_gather | solution.py:184
  144.9 1.3 collective-permute-start.4
  146.2 5.3 %collective-permute-start.3 = (bf16[64,64]{0,1:T(8,128)(2,1)S(1)}, bf16[64,64]{0,1:T(8,128)(2,1)S(1)}, u32[]{:S(2)}, u32[]{:S(2)}) collective-permute-start(bf16[64,64]{0,1:T(8,128)(2,1)S(1)} %dynamic-slice_bitcast_fusion.15), channel_id=1, source_target_pairs={{0,4},{4,8},{8,12},{12,16},{16,20},{20,24},{24,28},{1,5},{5,9},{9,... | collective-permute-start | bytes 24584 | tf_op jit(solution)/shard_map/ppermute | solution.py:15
  153.7 1.3 copy-done.2
  155.0 4.3 copy.622
  160.4 1.7 convert_reduce_fusion.1
  165.1 1.3 collective-permute-start.6
  167.1 6.2 %collective-permute-start.5 = (bf16[16,64]{1,0:T(8,128)(2,1)}, bf16[16,64]{1,0:T(8,128)(2,1)}, u32[]{:S(2)}, u32[]{:S(2)}) collective-permute-start(bf16[16,64]{1,0:T(8,128)(2,1)} %bitcast.119), channel_id=1, source_target_pairs={{0,4},{4,8},{8,12},{12,16},{16,20},{20,24},{24,28},{1,5},{5,9},{9,... | collective-permute-start | bytes 6152 | tf_op jit(solution)/shard_map/ppermute | solution.py:15
  180.7 1.3 copy-done.3
  181.9 4.3 copy.641
  186.2 1.3 reshape.876
  189.1 19.9 %reduce-scatter.3.cloned.1.call-done = bf16[2,16,512]{2,1,0:T(8,128)(2,1)} async-done(((bf16[2,64,512]{2,1,0:T(8,128)(2,1)}), bf16[2,16,512]{2,1,0:T(8,128)(2,1)}) %reduce-scatter.3.cloned.1.call-update) | async-done | bytes 32784 | tf_op jit(solution)/shard_map/reduce_scatter | solution.py:226
  210.2 3.6 collective-permute-start.7
  215.8 1.3 copy.669
  218.3 2.4 broadcast_in_dim.237
  220.7 2.8 copy.649
  224.5 1.7 copy.650
  226.2 3.4 fusion.73
  234.1 4.2 collective-permute-start.8
  239.4 1.3 collective-permute-start.9
  243.1 3.8 collective-permute-done.9
  249.0 98.3 %while.34 = (s32[]{:T(128)}, bf16[16,64,512]{2,0,1:T(8,128)(2,1)S(1)}, bf16[16,16,8,8,8]{1,4,3,2,0:T(8,128)(2,1)}, bf16[16,6,16,64]{3,2,1,0:T(8,128)(2,1)}, bf16[64,112]{1,0:T(8,128)(2,1)S(1)}) while((s32[]{:T(128)}, bf16[16,64,512]{2,0,1:T(8,128)(2,1)S(1)}, bf16[16,16,8,8,8]{1,4,3,2,0:T(8,128)(2,1)}, ...), condition=%wide.region_7.8_spmd.clone, body=%wide.region_6.7_spmd.sunk.clone | while | flops 7536647 | bytes 3061913 | solution.py:119
  260.1 1.2 dynamic_update_slice.21
  266.2 1.2 dynamic_update_slice.21
  272.4 1.2 dynamic_update_slice.21
  297.0 1.2 dynamic_update_slice.21
  303.1 1.2 dynamic_update_slice.21
  348.4 76.7 %while.35 = (s32[]{:T(128)}, f32[16,16,448]{2,1,0:T(8,128)}, bf16[16,16,512]{2,1,0:T(8,128)(2,1)S(1)}, bf16[16,64,8,8,8]{1,4,3,2,0:T(8,128)(2,1)}, bf16[16,6,64,64]{2,3,1,0:T(8,128)(2,1)}) while((s32[]{:T(128)}, f32[16,16,448]{2,1,0:T(8,128)}, bf16[16,16,512]{2,1,0:T(8,128)(2,1)S(1)}, bf16[16,64,8,8,8]{1,4,3,2,0:T(8,128)(2,1)}, ...), condition=%wide.region_10.11_spmd.clone, body=%wide.region_9.10_spmd.sunk.clone | while | flops 8126471 | bytes 5194901 | solution.py:257
  426.3 36.7 %all-reduce.8 = (f32[7,16,64]{2,0,1:T(8,128)S(1)}, f32[16]{0:T(128)S(1)}, f32[7,16,64]{2,1,0:T(8,128)S(1)}, f32[16]{0:T(128)S(1)}) all-reduce(f32[7,16,64]{2,0,1:T(8,128)S(1)} %bitcast.595, f32[16]{0:T(128)S(1)} %copy-done.20, f32[7,16,64]{2,1,0:T(8,128)S(1)} %convolution_bitcast_fusion.3, ...), channel_id=1, replica_groups=mesh['blocks'=8,'chan'=4] {'blocks'}, use_global_device_ids=true, to_apply=%region_12.13 | all-reduce | flops 14368 | bytes 114944 | tf_op jit(solution)/shard_map/psum | solution.py:270
  465.4 1.8 select_convert_fusion
  (1122 shorter events, 284.8 us)
Async XLA Ops:
  7.2 22.4 %all-gather.2.cloned.1.call-start = ((), (), s32[]{:S(2)}) async-start(), calls=%async_computation.2 | async-start | bytes 1310720 | tf_op jit(solution)/shard_map/all_gather | solution.py:161
  9.0 200.0 %reduce-scatter.3.cloned.1.call-start = ((), (), s32[]{:S(2)}) async-start(), calls=%async_computation.3 | async-start | bytes 163840 | tf_op jit(solution)/shard_map/reduce_scatter | solution.py:226
  25.1 127.0 %copy-start.13 = (s32[1024]{0:T(1024)}, s32[1024]{0:T(1024)S(1)}, u32[]{:S(2)}) copy-start(s32[1024]{0:T(1024)S(1)} %pad_clamp_fusion.2) | copy-start | bytes 12292
  25.1 127.7 %copy-start.12 = (s32[1024]{0:T(1024)}, s32[1024]{0:T(1024)S(1)}, u32[]{:S(2)}) copy-start(s32[1024]{0:T(1024)S(1)} %pad_clamp_fusion.3) | copy-start | bytes 12292
  40.8 7.9 %collective-permute-start = (bf16[4,3,64,64]{3,2,1,0:T(8,128)(2,1)S(1)}, bf16[4,3,64,64]{3,2,1,0:T(8,128)(2,1)}, u32[]{:S(2)}, u32[]{:S(2)}) collective-permute-start(bf16[4,3,64,64]{3,2,1,0:T(8,128)(2,1)S(1)} %constant_dynamic-slice_fusion.9), channel_id=1, source_target_pairs={{0,4},{4,8},{8,12},{12,16},{16,20},{20,24},{24,28},{1,5},{5,9},{9,... | collective-permute-start | bytes 294920 | tf_op jit(solution)/shard_map/ppermute | solution.py:15
  44.8 107.8 %copy-start.15 = (pred[2]{0:T(512)(128)(4,1)}, pred[2]{0:T(512)(128)(4,1)S(1)}, u32[]{:S(2)}) copy-start(pred[2]{0:T(512)(128)(4,1)S(1)} %get-tuple-element.353) | copy-start | bytes 10
  44.8 108.6 %copy-start.14 = (pred[2]{0:T(512)(128)(4,1)}, pred[2]{0:T(512)(128)(4,1)S(1)}, u32[]{:S(2)}) copy-start(pred[2]{0:T(512)(128)(4,1)S(1)} %get-tuple-element.354) | copy-start | bytes 10
  45.9 9.0 %collective-permute-start.1 = (bf16[4,3,64,64]{3,2,1,0:T(8,128)(2,1)}, bf16[4,3,64,64]{3,2,1,0:T(8,128)(2,1)}, u32[]{:S(2)}, u32[]{:S(2)}) collective-permute-start(bf16[4,3,64,64]{3,2,1,0:T(8,128)(2,1)} %slice.398), channel_id=1, source_target_pairs={{4,0},{8,4},{12,8},{16,12},{20,16},{24,20},{28,24},{5,1},{9,5},{13... | collective-permute-start | bytes 294920 | tf_op jit(solution)/shard_map/ppermute | solution.py:15
  58.3 65.4 %copy-start.16 = (f32[16]{0:T(128)S(1)}, f32[16]{0:T(128)}, u32[]{:S(2)}) copy-start(f32[16]{0:T(128)} %param.19) | copy-start | bytes 196
  123.6 5.3 %copy-start = (bf16[16,6,64,64]{2,3,1,0:T(8,128)(2,1)}, bf16[16,6,64,64]{2,3,1,0:T(8,128)(2,1)S(1)}, u32[]{:S(2)}) copy-start(bf16[16,6,64,64]{2,3,1,0:T(8,128)(2,1)S(1)} %get-tuple-element.676) | copy-start | bytes 2359300
  128.9 4.3 copy-start.10
  131.9 5.8 %collective-permute-start.2 = (bf16[7,16,64]{2,1,0:T(8,128)(2,1)S(1)}, bf16[7,16,64]{2,1,0:T(8,128)(2,1)S(1)}, u32[]{:S(2)}, u32[]{:S(2)}) collective-permute-start(bf16[7,16,64]{2,1,0:T(8,128)(2,1)S(1)} %copy.607), channel_id=1, source_target_pairs={{4,0},{8,4},{12,8},{16,12},{20,16},{24,20},{28,24},{5,1},{9,5},{13... | collective-permute-start | bytes 43016 | tf_op jit(solution)/shard_map/ppermute | solution.py:15
  133.2 27.2 %copy-start.21 = (pred[2]{0:T(512)(128)(4,1)}, pred[2]{0:T(512)(128)(4,1)S(1)}, u32[]{:S(2)}) copy-start(pred[2]{0:T(512)(128)(4,1)S(1)} %iota_compare_fusion.1) | copy-start | bytes 10
  144.9 7.1 %collective-permute-start.4 = (bf16[64,64]{0,1:T(8,128)(2,1)S(1)}, bf16[64,64]{0,1:T(8,128)(2,1)S(1)}, u32[]{:S(2)}, u32[]{:S(2)}) collective-permute-start(bf16[64,64]{0,1:T(8,128)(2,1)S(1)} %slice_bitcast_fusion.19), channel_id=1, source_target_pairs={{4,0},{8,4},{12,8},{16,12},{20,16},{24,20},{28,24},{5,1},{9,5},{13... | collective-permute-start | bytes 24584 | tf_op jit(solution)/shard_map/ppermute | solution.py:15
  146.2 6.6 %collective-permute-start.3 = (bf16[64,64]{0,1:T(8,128)(2,1)S(1)}, bf16[64,64]{0,1:T(8,128)(2,1)S(1)}, u32[]{:S(2)}, u32[]{:S(2)}) collective-permute-start(bf16[64,64]{0,1:T(8,128)(2,1)S(1)} %dynamic-slice_bitcast_fusion.15), channel_id=1, source_target_pairs={{0,4},{4,8},{8,12},{12,16},{16,20},{20,24},{24,28},{1,5},{5,9},{9,... | collective-permute-start | bytes 24584 | tf_op jit(solution)/shard_map/ppermute | solution.py:15
  153.7 1.3 copy-start.2
  159.3 1.1 copy-start.24
  159.3 1.1 copy-start.25
  162.1 3.0 copy-start.8
  165.1 10.7 %collective-permute-start.6 = (bf16[16,64]{0,1:T(8,128)(2,1)S(1)}, bf16[16,64]{0,1:T(8,128)(2,1)S(1)}, u32[]{:S(2)}, u32[]{:S(2)}) collective-permute-start(bf16[16,64]{0,1:T(8,128)(2,1)S(1)} %slice_bitcast_fusion.18), channel_id=1, source_target_pairs={{4,0},{8,4},{12,8},{16,12},{20,16},{24,20},{28,24},{5,1},{9,5},{13... | collective-permute-start | bytes 6152 | tf_op jit(solution)/shard_map/ppermute | solution.py:15
  167.1 8.4 %copy-start.7 = (bf16[2,16,8,7,8]{1,4,3,2,0:T(8,128)(2,1)S(1)}, bf16[2,16,8,7,8]{1,4,3,2,0:T(8,128)(2,1)}, u32[]{:S(2)}) copy-start(bf16[2,16,8,7,8]{1,4,3,2,0:T(8,128)(2,1)} %get-tuple-element.324) | copy-start | bytes 86020
  167.1 10.3 %collective-permute-start.5 = (bf16[16,64]{1,0:T(8,128)(2,1)}, bf16[16,64]{1,0:T(8,128)(2,1)}, u32[]{:S(2)}, u32[]{:S(2)}) collective-permute-start(bf16[16,64]{1,0:T(8,128)(2,1)} %bitcast.119), channel_id=1, source_target_pairs={{0,4},{4,8},{8,12},{12,16},{16,20},{20,24},{24,28},{1,5},{5,9},{9,... | collective-permute-start | bytes 6152 | tf_op jit(solution)/shard_map/ppermute | solution.py:15
  173.2 7.3 %copy-start.6 = (bf16[2,16,7,8,8]{1,4,3,2,0:T(8,128)(2,1)S(1)}, bf16[2,16,7,8,8]{1,4,3,2,0:T(8,128)(2,1)}, u32[]{:S(2)}) copy-start(bf16[2,16,7,8,8]{1,4,3,2,0:T(8,128)(2,1)} %get-tuple-element.320) | copy-start | bytes 86020
  180.6 1.3 copy-start.3
  186.2 22.8 %copy-start.22 = (pred[2]{0:T(512)(128)(4,1)S(1)}, pred[2]{0:T(512)(128)(4,1)}, u32[]{:S(2)}) copy-start(pred[2]{0:T(512)(128)(4,1)} %copy-done.21) | copy-start | bytes 10
  186.2 28.8 %copy-start.11 = (bf16[7,16,64]{2,1,0:T(8,128)(2,1)S(1)}, bf16[7,16,64]{2,1,0:T(8,128)(2,1)}, u32[]{:S(2)}) copy-start(bf16[7,16,64]{2,1,0:T(8,128)(2,1)} %param.18) | copy-start | bytes 43012
  188.5 276.9 %reduce-scatter.5.cloned.1.call-start = ((), (), s32[]{:S(2)}) async-start(), calls=%async_computation.4 | async-start | bytes 1310720 | tf_op jit(solution)/shard_map/reduce_scatter | solution.py:266
  210.2 7.1 %collective-permute-start.7 = (bf16[7,16,64]{1,2,0:T(8,128)(2,1)S(1)}, bf16[7,16,64]{1,2,0:T(8,128)(2,1)S(1)}, u32[]{:S(2)}, u32[]{:S(2)}) collective-permute-start(bf16[7,16,64]{1,2,0:T(8,128)(2,1)S(1)} %constant_dynamic-slice_fusion.7), channel_id=1, source_target_pairs={{0,4},{4,8},{8,12},{12,16},{16,20},{20,24},{24,28},{1,5},{5,9},{9,... | collective-permute-start | bytes 43016 | tf_op jit(solution)/shard_map/ppermute | solution.py:15
  214.4 9.1 %copy-start.18 = (pred[16]{0:T(512)(128)(4,1)}, pred[16]{0:T(512)(128)(4,1)S(1)}, u32[]{:S(2)}) copy-start(pred[16]{0:T(512)(128)(4,1)S(1)} %iota_compare_fusion) | copy-start | bytes 52
  220.7 2.9 copy-start.4
  220.7 2.9 copy-start.17
  233.9 4.4 copy-start.1
  233.9 4.4 copy-start.9
  234.1 6.9 %collective-permute-start.8 = (bf16[4,3,16,64]{2,3,1,0:T(8,128)(2,1)S(1)}, bf16[4,3,16,64]{2,3,1,0:T(8,128)(2,1)}, u32[]{:S(2)}, u32[]{:S(2)}) collective-permute-start(bf16[4,3,16,64]{2,3,1,0:T(8,128)(2,1)S(1)} %constant_dynamic-slice_fusion.6), channel_id=1, source_target_pairs={{0,4},{4,8},{8,12},{12,16},{16,20},{20,24},{24,28},{1,5},{5,9},{9,... | collective-permute-start | bytes 73736 | tf_op jit(solution)/shard_map/ppermute | solution.py:15
  239.4 7.6 %collective-permute-start.9 = (bf16[4,3,16,64]{2,3,1,0:T(8,128)(2,1)S(1)}, bf16[4,3,16,64]{2,3,1,0:T(8,128)(2,1)S(1)}, u32[]{:S(2)}, u32[]{:S(2)}) collective-permute-start(bf16[4,3,16,64]{2,3,1,0:T(8,128)(2,1)S(1)} %slice.436), channel_id=1, source_target_pairs={{4,0},{8,4},{12,8},{16,12},{20,16},{24,20},{28,24},{5,1},{9,5},{13... | collective-permute-start | bytes 73736 | tf_op jit(solution)/shard_map/ppermute | solution.py:15
  347.4 1.0 copy-start.5
  348.4 77.9 %copy-start.20 = (f32[16]{0:T(128)S(1)}, f32[16]{0:T(128)}, u32[]{:S(2)}) copy-start(f32[16]{0:T(128)} %get-tuple-element.268) | copy-start | bytes 196
  348.4 77.9 %copy-start.23 = (f32[16]{0:T(128)S(1)}, f32[16]{0:T(128)}, u32[]{:S(2)}) copy-start(f32[16]{0:T(128)} %get-tuple-element.266) | copy-start | bytes 196
  348.4 117.0 %copy-start.19 = (pred[16]{0:T(512)(128)(4,1)S(1)}, pred[16]{0:T(512)(128)(4,1)}, u32[]{:S(2)}) copy-start(pred[16]{0:T(512)(128)(4,1)} %copy-done.18) | copy-start | bytes 52
Sparse Core Ops, SparseCore 0:
  10.1 19.4 all-gather.1
  188.6 20.3 reduce-scatter.2
  348.5 24.6 reduce-scatter.4
where the time goes:
time: 478 us; the launch traced here: 474 us
  local copies, waits for them, and re-layouts  260 us (54%)
  other arithmetic  47 us (10%)
  blocking collectives  42.1 us (9%)
  waiting for transfers between devices  37 us (8%)
  matrix products  31.9 us (7%)
  starting transfers between devices  29.9 us (6%)
  between operations  21.3 us (4%)
    another operation x48, local copies, waits for them, and re-layouts, block_views(): jnp.stack([block_cube, minus_x, plus_x, minus_y, plus_y, minus_z, plus_z])  52.6 us
    squeeze x48, local copies, waits for them, and re-layouts, apply_blocks(): return lax.map(one_block, (block_cubes, halo_table))  45.5 us
    psum x1, blocking collectives, local(): lax.psum((fine_weight_grad, fine_bias_grad), 'blocks')  36.7 us
    ppermute x10, starting transfers between devices, from_behind(): return lax.ppermute(block, axis, route)  29.8 us
    reshape x50, local copies, waits for them, and re-layouts, block_views(): return stacked.reshape(7 * channels, edge_cells ** 3)  28.9 us
    dynamic_update_slice x32, local copies, waits for them, and re-layouts, apply_blocks(): return lax.map(one_block, (block_cubes, halo_table))  20.9 us
    reduce_scatter x1, waiting for transfers between devices, local(): lax.psum_scatter(partial_sums.astype(jnp.bfloat16), 'chan', scatter_dimen...  19.9 us
    while x240, other arithmetic  17.3 us
  transfers between devices with their start and end apart: 13, of which 8 were waited for; matrix products, arithmetic and copies ran while one was open for 22% of the time, Pallas kernels for 0%

commit v1 on v0

v1 whole, which is shorter than its diff:
```python
import jax
import jax.numpy as jnp
import numpy as np
from jax import lax
from jax.experimental import pallas as pl
from jax.experimental.pallas import tpu as pltpu
from jax.sharding import PartitionSpec as P

EDGE = 8
CELLS = EDGE**3
TAP_PAIRS = (0, 2, 1, 4, 3, 6, 5)
STRIDES = (1, 8, 64)
F32 = jnp.float32
BF16 = jnp.bfloat16


def from_behind(block, axis, distance):
    devices = range(lax.axis_size(axis))
    route = [(i - distance, i) for i in devices if i - distance in devices]
    return lax.ppermute(block, axis, route)


def octant_maps():
    z, y, x = np.meshgrid(*[np.arange(EDGE)] * 3, indexing="ij")
    spread = np.zeros((8, CELLS, CELLS), np.float32)
    pool = np.zeros((CELLS, 64), np.float32)
    place = np.zeros((8, 64, CELLS), np.float32)
    fine = np.arange(CELLS)
    small = ((z // 2) * 16 + (y // 2) * 4 + x // 2).reshape(-1)
    pool[fine, small] = 1.0
    for q in range(8):
        cz, cy, cx = z // 2 + 4 * (q // 4), y // 2 + 4 * (q // 2 % 2), x // 2 + 4 * (q % 2)
        coarse = (cz * 64 + cy * 8 + cx).reshape(-1)
        spread[q, coarse, fine] = 1.0
        place[q, small, coarse] = 1.0
    return spread, pool, place


def paired(taps):
    return jnp.stack([taps[t] for t in TAP_PAIRS])


def sigmoid(v):
    return 1.0 / (1.0 + jnp.exp(-v))


def write_views(views, own, neighbours, width):
    lane = lax.broadcasted_iota(jnp.int32, own.shape, 1)
    views[0:width, :] = own
    wide = own.astype(F32)
    for axis in range(3):
        stride = STRIDES[axis]
        coord = lane // stride % EDGE
        for side in range(2):
            near, far = (0, EDGE - 1) if side == 0 else (EDGE - 1, 0)
            step = stride if side == 0 else CELLS - stride
            wrap = (CELLS - 7 * stride) if side == 0 else 7 * stride
            tap = 1 + 2 * axis + side
            other = neighbours[2 * axis + side]
            if other is None:
                out = jnp.where(coord == near, 0.0, pltpu.roll(wide, step, 1))
            else:
                mixed = jnp.where(coord == far, other.astype(F32), wide)
                out = pltpu.roll(mixed, step, 1)
                if step != wrap % CELLS:
                    out = jnp.where(coord == near, pltpu.roll(mixed, wrap, 1), out)
            views[tap * width : (tap + 1) * width, :] = out.astype(BF16)


def forward_kernel(near, table, weight, bias, pool, slope, octants, views):
    width = table.shape[1]

    def row(j, carry):
        own = table[j + 4]
        write_views(views, own, [table[near[j * 6 + n]] for n in range(6)], width)
        v = jnp.dot(weight[...], views[...], preferred_element_type=F32) + bias[...]
        s = sigmoid(v)
        slope[j] = s * (1.0 + v * (1.0 - s))

        @pl.when(jnp.logical_and(j >= 4, j < 20))
        def _():
            hidden = (v * s).astype(BF16)
            small = jnp.dot(hidden, pool[...], preferred_element_type=F32) * 0.125
            octants[j - 4] = small.astype(BF16)

        return carry

    lax.fori_loop(0, slope.shape[0], row, 0)


def backward_kernel(
    near, facts, octant_at, cotangent_at, table, slope, octants, cotangent, forward_w, coarse_b, back_coarse_w, back_w,
    place, spread,
    coarse_out, fine_grad, fine_wg, fine_bg, coarse_wg, coarse_bg,
    views, coarse_in, coarse_act, coarse_delta, coarse_back, fine_delta, bias_sum,
):
    width = table.shape[1]
    group = fine_grad.shape[1]
    chan, live, parent0, coarse_row, coarse_live = (facts[n] for n in range(5))
    mine = pl.ds(pl.multiple_of(chan * group, group), group)

    def own_views():
        return jnp.concatenate(
            [views[pl.ds(pl.multiple_of(t * width + chan * group, group), group), :] for t in range(7)],
            axis=0,
        )

    def assemble(k, carry):
        total = jnp.zeros((width, CELLS), F32)
        for q in range(8):
            total += jnp.dot(
                octants[octant_at[k * 8 + q]], place[q], preferred_element_type=F32
            )
        inside = jnp.logical_and(k >= facts[5], k < facts[6])
        coarse_in[k] = jnp.where(inside, total, 0.0).astype(BF16)
        return carry

    lax.fori_loop(0, 8, assemble, 0)

    def coarse_forward(k, carry):
        write_views(
            views, coarse_in[k + 1], [None] * 4 + [coarse_in[k], coarse_in[k + 2]], width
        )
        v = jnp.dot(forward_w[...], views[...], preferred_element_type=F32) + coarse_b[...]
        s = sigmoid(v)
        coarse_act[k] = (v * s).astype(BF16)
        inside = jnp.logical_and(k + 1 >= facts[5], k + 1 < facts[6])
        delta = cotangent[cotangent_at[k]].astype(F32) * (s * (1.0 + v * (1.0 - s)))
        coarse_delta[k] = jnp.where(inside, delta, 0.0).astype(BF16)
        return carry

    lax.fori_loop(0, 6, coarse_forward, 0)
    for s in range(coarse_out.shape[0]):
        row = jnp.minimum(coarse_row + s, 5)
        kept = jnp.where(s < coarse_live, coarse_act[row, mine, :].astype(F32), 0.0)
        coarse_out[s] = kept.astype(BF16)

    coarse_wg[...] = jnp.zeros_like(coarse_wg)
    bias_sum[...] = jnp.zeros_like(bias_sum)

    def coarse_backward(k, carry):
        write_views(
            views,
            coarse_delta[k + 1],
            [None] * 4 + [coarse_delta[k], coarse_delta[k + 2]],
            width,
        )
        coarse_back[k] = jnp.dot(
            back_coarse_w[...], views[...], preferred_element_type=F32
        ).astype(BF16)
        row = k + 1

        @pl.when(jnp.logical_and(row >= coarse_row, row < coarse_row + coarse_live))
        def _():
            coarse_wg[...] += lax.dot_general(
                own_views(), coarse_in[k + 2], (((1,), (1,)), ((), ())), preferred_element_type=F32
            )
            bias_sum[...] += coarse_delta[row, mine, :].astype(F32)

        return carry

    lax.fori_loop(0, 4, coarse_backward, 0)
    coarse_bg[...] = jnp.broadcast_to(
        jnp.sum(bias_sum[...], axis=1, keepdims=True), coarse_bg.shape
    )

    def delta_row(j, carry):
        index = parent0 + j
        up = jnp.dot(coarse_back[index // 8], spread[index % 8], preferred_element_type=F32)
        fine_delta[j] = (up * 0.125 * slope[j]).astype(BF16)
        return carry

    lax.fori_loop(0, slope.shape[0], delta_row, 0)
    fine_delta[slope.shape[0]] = jnp.zeros((width, CELLS), BF16)
    fine_wg[...] = jnp.zeros_like(fine_wg)
    bias_sum[...] = jnp.zeros_like(bias_sum)

    def fine_row(r, carry):
        @pl.when(r < live)
        def _():
            write_views(
                views, fine_delta[r + 4], [fine_delta[near[r * 6 + n]] for n in range(6)], width
            )
            fine_grad[r] = jnp.dot(back_w[...], views[...], preferred_element_type=F32).astype(BF16)
            fine_wg[...] += lax.dot_general(
                own_views(), table[r + 8], (((1,), (1,)), ((), ())), preferred_element_type=F32
            )
            bias_sum[...] += fine_delta[r + 4, mine, :].astype(F32)

        @pl.when(r >= live)
        def _():
            fine_grad[r] = jnp.zeros((group, CELLS), BF16)

        return carry

    lax.fori_loop(0, fine_grad.shape[0], fine_row, 0)
    fine_bg[...] = jnp.broadcast_to(jnp.sum(bias_sum[...], axis=1, keepdims=True), fine_bg.shape)


def local(
    fine_input, block_counts, fine_weight, fine_bias, coarse_weight, coarse_bias, coarse_cotangent
):
    slots, group, cells = fine_input.shape
    coarse_slots = coarse_cotangent.shape[0]
    channels = fine_weight.shape[2]
    device = lax.axis_index("blocks")
    chan = lax.axis_index("chan")
    order = jnp.arange(block_counts.shape[0])
    earlier = order[None, :] < order[:, None]
    starts = jnp.sum(jnp.where(earlier, block_counts[None, :], 0), axis=1)
    first = starts[device]
    live = block_counts[device]
    total = jnp.sum(block_counts)
    coarse_total = total // 8
    coarse_first = (first + 7) // 8
    coarse_count = (first + live + 7) // 8 - coarse_first

    lower = from_behind(lax.dynamic_slice_in_dim(fine_input, live - 8, 8, 0), "blocks", 1)
    upper = from_behind(fine_input[:8], "blocks", -1)
    rows = slots + 16
    table = jnp.concatenate([lower, fine_input, jnp.zeros((9, group, cells), BF16)], axis=0)
    table = lax.dynamic_update_slice_in_dim(table, upper, 8 + live, 0)
    table = lax.all_gather(table, "chan", axis=1, tiled=True)
    weights = lax.all_gather(
        jnp.concatenate([fine_weight, coarse_weight]), "chan", axis=1, tiled=True
    )
    biases = lax.all_gather(jnp.stack([fine_bias, coarse_bias]), "chan", axis=1, tiled=True)
    cotangents = lax.all_gather(
        lax.all_gather(coarse_cotangent, "chan", axis=1, tiled=True), "blocks", axis=0, tiled=True
    )
    full_fine, full_coarse = weights[:7], weights[7:]

    spread, pool, place = (jnp.asarray(a, BF16) for a in octant_maps())
    delta_rows = slots + 8
    ids = first - 4 + jnp.arange(delta_rows, dtype=jnp.int32)
    px, py = ids % 2, ids // 2 % 2
    valid = jnp.stack(
        [px == 1, px == 0, py == 1, py == 0, ids >= 4, ids + 4 < total], axis=1
    )
    offsets = jnp.array([-1, 1, -2, 2, -4, 4], jnp.int32)[None, :]
    spot = jnp.arange(delta_rows, dtype=jnp.int32)[:, None] + offsets
    near_fine = jnp.where(valid, spot + 4, rows).reshape(-1)
    near_delta = jnp.where(valid, spot, delta_rows)[4 : 4 + slots].reshape(-1)

    smem = pl.BlockSpec(memory_space=pltpu.SMEM)
    vmem = pl.BlockSpec(memory_space=pltpu.VMEM)
    slope, octants = pl.pallas_call(
        forward_kernel,
        out_shape=(
            jax.ShapeDtypeStruct((delta_rows, channels, cells), F32),
            jax.ShapeDtypeStruct((slots, channels, 64), BF16),
        ),
        in_specs=[smem] + [vmem] * 4,
        out_specs=(vmem, vmem),
        scratch_shapes=[pltpu.VMEM((7 * channels, cells), BF16)],
        compiler_params=pltpu.CompilerParams(vmem_limit_bytes=40 * 2**20),
    )(
        near_fine,
        table,
        full_fine.transpose(1, 0, 2).reshape(channels, 7 * channels),
        biases[0][:, None],
        pool,
    )

    every_octant = lax.all_gather(octants, "blocks", axis=0, tiled=True)
    parent = (first - 4) // 8

    def owner_of(block):
        below = starts[None, :] <= block[:, None]
        return (
            jnp.sum(below.astype(jnp.int32), axis=1) - 1,
            jnp.max(jnp.where(below, starts[None, :], 0), axis=1),
        )

    octant_ids = (parent - 2) * 8 + jnp.arange(64, dtype=jnp.int32)
    safe = jnp.clip(octant_ids, 0, total - 1)
    owner, start = owner_of(safe)
    octant_at = owner * slots + safe - start
    coarse_ids = parent - 1 + jnp.arange(6, dtype=jnp.int32)
    safe = jnp.clip(coarse_ids, 0, coarse_total - 1)
    owner, start = owner_of(safe * 8)
    cotangent_at = owner * coarse_slots + safe - (start + 7) // 8

    facts = jnp.stack(
        [
            chan,
            live,
            first - 4 - parent * 8,
            coarse_first - parent + 1,
            coarse_count,
            2 - parent,
            coarse_total - parent + 2,
        ]
    ).astype(jnp.int32)
    back_coarse = paired(full_coarse).transpose(2, 0, 1).reshape(channels, 7 * channels)
    back_fine = paired(full_fine).transpose(2, 0, 1).reshape(channels, 7 * channels)
    back_fine = lax.dynamic_slice_in_dim(back_fine, chan * group, group, 0)
    coarse_out, fine_grad, fine_wg, fine_bg, coarse_wg, coarse_bg = pl.pallas_call(
        backward_kernel,
        out_shape=(
            jax.ShapeDtypeStruct((coarse_slots, group, cells), BF16),
            jax.ShapeDtypeStruct((slots, group, cells), BF16),
            jax.ShapeDtypeStruct((7 * group, channels), F32),
            jax.ShapeDtypeStruct((group, channels), F32),
            jax.ShapeDtypeStruct((7 * group, channels), F32),
            jax.ShapeDtypeStruct((group, channels), F32),
        ),
        in_specs=[smem] * 4 + [vmem] * 10,
        out_specs=(vmem,) * 6,
        scratch_shapes=[
            pltpu.VMEM((7 * channels, cells), BF16),
            pltpu.VMEM((8, channels, cells), BF16),
            pltpu.VMEM((6, channels, cells), BF16),
            pltpu.VMEM((6, channels, cells), BF16),
            pltpu.VMEM((4, channels, cells), BF16),
            pltpu.VMEM((delta_rows + 1, channels, cells), BF16),
            pltpu.VMEM((group, cells), F32),
        ],
        compiler_params=pltpu.CompilerParams(vmem_limit_bytes=56 * 2**20),
    )(
        near_delta,
        facts,
        octant_at,
        cotangent_at,
        table,
        slope,
        every_octant,
        cotangents,
        full_coarse.transpose(1, 0, 2).reshape(channels, 7 * channels),
        biases[1][:, None],
        back_coarse,
        back_fine,
        place,
        spread,
    )
    partial = jnp.concatenate([fine_wg, fine_bg, coarse_wg, coarse_bg], axis=0)
    sums = jnp.sum(lax.all_gather(partial, "blocks", axis=0), axis=0)
    half = 8 * group
    fine_norm = jnp.sqrt(total.astype(F32) * cells)
    coarse_norm = jnp.sqrt(coarse_total.astype(F32) * cells)
    fine_sums = sums[:half] / fine_norm
    coarse_sums = sums[half:] / coarse_norm

    def weight_part(part):
        return paired(part[: 7 * group].reshape(7, group, channels))

    return (
        coarse_out,
        fine_grad,
        weight_part(fine_sums),
        fine_sums[7 * group :, 0],
        weight_part(coarse_sums),
        coarse_sums[7 * group :, 0],
    )


def solution(mesh):
    placed = (
        P("blocks", "chan", None),
        P(),
        P(None, "chan", None),
        P("chan"),
        P(None, "chan", None),
        P("chan"),
        P("blocks", "chan", None),
    )
    return jax.shard_map(
        local,
        mesh=mesh,
        in_specs=placed,
        out_specs=(
            P("blocks", "chan", None),
            P("blocks", "chan", None),
            P(None, "chan", None),
            P("chan"),
            P(None, "chan", None),
            P("chan"),
        ),
        check_vma=False,
    )
```

time: 478 us -> 207 us (0.43)
  local copies, waits for them, and re-layouts: 260 us -> 14.7 us
  other arithmetic: 47 us -> 8.37 us
  Pallas kernels: 0 us -> 37.3 us
  matrix products: 31.9 us -> 0 us
  waiting for transfers between devices: 37 us -> 66.5 us
  starting transfers between devices: 29.9 us -> 6.26 us
  blocking collectives: 42.1 us -> 51 us
    squeeze x183 -> x0, local copies, waits for them, and re-layouts: 61.5 us -> none  [the longest x48 45.5 us: apply_blocks(): return lax.map(one_block, (block_cubes, halo_table))]
    all_gather x1 -> x3, waiting for transfers between devices: 3.81 us -> 62.6 us  [the longest x1 50.8 us: local(): every_octant = lax.all_gather(octants, 'blocks', axis=0, tiled=True)]
    another operation x55 -> x8, local copies, waits for them, and re-layouts: 55.7 us -> 2.09 us  [the longest x1 1.24 us: local(): jnp.stack([chan, live, first - 4 - parent * 8, coarse_first - parent + 1,...]
    all_gather x1 -> x4, blocking collectives: 5.42 us -> 51 us  [the longest x1 33.3 us: local(): sums = jnp.sum(lax.all_gather(partial, 'blocks', axis=0), axis=0)]
    pallas_call x0 -> x2, Pallas kernels: none -> 37.3 us  [the longest x1 22.9 us: local(): pl.pallas_call(backward_kernel, out_shape=(jax.ShapeDtypeStruct((coarse_s...]
    psum x1 -> x0, blocking collectives: 36.7 us -> none  [local(): lax.psum((fine_weight_grad, fine_bias_grad), 'blocks')]
    dot_general x51 -> x0, matrix products: 31.9 us -> none  [the longest x32 16.3 us: one_block(): jnp.dot(matrix, block_views(operands[0], operands[1]), preferred_element_...]
    reshape x58 -> x4, local copies, waits for them, and re-layouts: 29.6 us -> 2.22 us  [the longest x1 0.76 us: local(): full_coarse.transpose(1, 0, 2).reshape(channels, 7 * channels)]
  transfers between devices with their start and end apart: 13 -> 5, of which waited for: 8 -> 4; matrix products, arithmetic and copies ran while one was open for 22% -> 7% of each run, Pallas kernels for 0% -> 7%
where the time goes in v1:
time: 207 us
  waiting for transfers between devices  66.5 us (32%)
  blocking collectives  51 us (25%)
  Pallas kernels  37.3 us (18%)
  between operations  22.7 us (11%)
  local copies, waits for them, and re-layouts  14.7 us (7%)
  other arithmetic  8.37 us (4%)
  starting transfers between devices  6.26 us (3%)
    all_gather x1, waiting for transfers between devices, local(): every_octant = lax.all_gather(octants, 'blocks', axis=0, tiled=True)  50.8 us
    all_gather x1, blocking collectives, local(): sums = jnp.sum(lax.all_gather(partial, 'blocks', axis=0), axis=0)  33.3 us
    pallas_call x1, Pallas kernels, local(): pl.pallas_call(backward_kernel, out_shape=(jax.ShapeDtypeStruct((coarse_s...  22.9 us
    pallas_call x1, Pallas kernels, local(): pl.pallas_call(forward_kernel, out_shape=(jax.ShapeDtypeStruct((delta_row...  14.4 us
    all_gather x1, waiting for transfers between devices, local(): lax.all_gather(lax.all_gather(coarse_cotangent, 'chan', axis=1, tiled=Tru...  11.8 us
    all_gather x1, blocking collectives, local(): lax.all_gather(coarse_cotangent, 'chan', axis=1, tiled=True)  6.96 us
    ppermute x2, starting transfers between devices, from_behind(): return lax.ppermute(block, axis, route)  6.14 us
    all_gather x1, blocking collectives, local(): lax.all_gather(jnp.concatenate([fine_weight, coarse_weight]), 'chan', axi...  5.7 us
  transfers between devices with their start and end apart: 5, of which 4 were waited for; matrix products, arithmetic and copies ran while one was open for 7% of the time, Pallas kernels for 7%

profile of v1, /device:TPU:0, one launch (start us, length us, event | category | flops | bytes accessed | tf_op | source)
XLA Modules:
  0.0 206.8 jit_solution(13556763944634875160)
XLA Ops:
  7.2 1.2 dynamic_slice.13
  9.8 1.0 fusion.8
  10.8 4.8 %collective-permute-start = (bf16[8,16,512]{2,1,0:T(8,128)(2,1)S(1)}, bf16[8,16,512]{2,1,0:T(8,128)(2,1)S(1)}, u32[]{:S(2)}, u32[]{:S(2)}) collective-permute-start(bf16[8,16,512]{2,1,0:T(8,128)(2,1)S(1)} %get-tuple-element.27), channel_id=1, source_target_pairs={{0,4},{4,8},{8,12},{12,16},{16,20},{20,24},{24,28},{1,5},{5,9},{9,... | collective-permute-start | bytes 393224 | tf_op jit(solution)/shard_map/ppermute | solution.py:20
  15.6 1.3 collective-permute-start.1
  17.7 0.7 collective-permute-done
  18.4 1.1 maximum_maximum_fusion
  19.4 3.1 %collective-permute-done.1 = bf16[8,16,512]{2,1,0:T(8,128)(2,1)S(1)} collective-permute-done((bf16[8,16,512]{2,1,0:T(8,128)(2,1)S(1)}, bf16[8,16,512]{2,1,0:T(8,128)(2,1)S(1)}, u32[]{:S(2)}, u32[]{:S(2)}) %collective-permute-start.1) | collective-permute-done | bytes 131104 | tf_op jit(solution)/shard_map/ppermute | solution.py:20
  22.5 0.8 copy-done.3
  23.4 7.0 %all_gather.28 = bf16[2,64,512]{2,1,0:T(8,128)(2,1)} all-gather(bf16[2,16,512]{2,1,0:T(8,128)(2,1)} %param.17), channel_id=1, replica_groups=mesh['blocks'=8,'chan'=4] {'chan'}, dimensions={1}, use_global_device_ids=true | all-gather | bytes 163840 | tf_op jit(solution)/shard_map/all_gather | solution.py:229
  30.5 1.3 reduce_sum.46
  35.7 0.8 select_reduce_fusion
  36.4 0.6 dynamic_slice.12
  39.8 0.7 maximum_bitcast_fusion
  40.5 5.1 %all-gather.1 = f32[4,16,2]{1,2,0:T(2,128)S(1)} all-gather(f32[1,16,2]{1,2,0:T(2,128)S(1)} %maximum_bitcast_fusion), channel_id=1, replica_groups=mesh['blocks'=8,'chan'=4] {'chan'}, dimensions={0}, use_global_device_ids=true | all-gather | bytes 640 | tf_op jit(solution)/shard_map/all_gather | solution.py:227
  45.5 0.1 reshape.218
  45.6 0.7 add_compare_fusion
  46.4 0.7 add_select_fusion
  47.2 0.1 copy.40
  47.2 0.6 reshape.211.near
  47.8 0.1 copy.41
  47.9 0.1 select_n.119.near
  48.0 0.7 copy.48.coarse_b
  48.7 0.1 copy.44.bias
  48.8 0.8 pad_maximum_fusion.1
  49.6 5.7 %all_gather.25 = bf16[14,64,64]{2,1,0:T(8,128)(2,1)S(1)} all-gather(bf16[14,16,64]{2,1,0:T(8,128)(2,1)S(1)} %pad_maximum_fusion.1), channel_id=1, replica_groups=mesh['blocks'=8,'chan'=4] {'chan'}, dimensions={1}, use_global_device_ids=true | all-gather | bytes 143360 | tf_op jit(solution)/shard_map/all_gather | solution.py:224
  55.3 0.1 copy.42
  55.4 0.1 reshape.212.weight
  55.7 1.6 copy-done
  57.3 14.4 %shard_map.154 = (f32[24,64,512]{2,1,0:T(8,128)S(1)}, bf16[16,64,64]{2,1,0:T(8,128)(2,1)}) custom-call(s32[144]{0:T(256)S(1)} %select_n.119.near, bf16[33,64,512]{2,1,0:T(8,128)(2,1)S(1)} %copy-done, bf16[64,448]{1,0:T(8,128)(2,1)S(1)} %reshape.212.weight, f32[64,1]{1,0:T(8,128)S(1)} %copy.44.bias, bf16[512,64]{1,0:T(8,128)(2,1)S(1)} %copy-done.2), custom_call_target="tpu_custom_call" | custom-call | tf_op jit(solution)/shard_map/pallas_call | solution.py:247
  71.7 1.6 copy-done.1
  73.4 0.1 constant_dynamic-slice_fusion.1
  73.5 0.7 copy.51.back_w
  74.2 0.7 copy.49.back_coarse_w
  74.9 0.1 copy.45
  75.0 0.8 reshape.213.forward_w
  75.8 1.2 stack.58.facts
  77.0 0.2 fusion.2
  77.2 0.1 fusion
  77.3 0.5 fusion.6.cotangent_at
  77.8 0.6 add_subtract_fusion.octant_at
  78.4 11.8 %all-gather.10.cloned.1.call-done.cotangent = bf16[16,64,512]{2,1,0:T(8,128)(2,1)} async-done(((bf16[2,64,512]{2,1,0:T(8,128)(2,1)}), bf16[16,64,512]{2,1,0:T(8,128)(2,1)}) %all-gather.10.cloned.1.call-update) | async-done | bytes 1048592 | tf_op jit(solution)/shard_map/all_gather | solution.py:228
  90.2 50.8 %all-gather.8.cloned.1.call-done.octants = bf16[128,64,64]{2,1,0:T(8,128)(2,1)} async-done(((bf16[16,64,64]{2,1,0:T(8,128)(2,1)}), bf16[128,64,64]{2,1,0:T(8,128)(2,1)}) %all-gather.8.cloned.1.call-update) | async-done | bytes 1048592 | tf_op jit(solution)/shard_map/all_gather | solution.py:265
  141.0 22.9 %shard_map.155 = (bf16[2,16,512]{2,1,0:T(8,128)(2,1)}, bf16[16,16,512]{2,1,0:T(8,128)(2,1)}, f32[112,64]{1,0:T(8,128)}, f32[16,64]{1,0:T(8,128)}, f32[112,64]{1,0:T(8,128)}, /*index=5*/f32[16,64]{1,0:T(8,128)}) custom-call(s32[96]{0:T(128)} %reshape.211.near, s32[7]{0:T(128)} %stack.58.facts, s32[64]{0:T(128)} %add_subtract_fusion.octant_at, ...), custom_call_target="tpu_custom_call" | custom-call | tf_op jit(solution)/shard_map/pallas_call | solution.py:298
  163.9 0.9 pad_maximum_fusion
  164.8 33.3 %all-gather = f32[2048,64]{1,0:T(8,128)S(1)} all-gather(f32[256,64]{1,0:T(8,128)S(1)} %pad_maximum_fusion), channel_id=2, replica_groups=mesh['blocks'=8,'chan'=4] {'blocks'}, dimensions={0}, use_global_device_ids=true | all-gather | bytes 589824 | tf_op jit(solution)/shard_map/all_gather | solution.py:337
  198.3 0.6 slice_reduce_fusion
  198.9 0.6 slice_reduce_fusion.1
  199.6 0.5 copy-done.5
  (50 shorter events, 0.8 us)
Async XLA Ops:
  7.2 48.5 %copy-start.2 = (bf16[512,64]{1,0:T(8,128)(2,1)S(1)}, bf16[512,64]{1,0:T(8,128)(2,1)}, u32[]{:S(2)}) copy-start(bf16[512,64]{1,0:T(8,128)(2,1)} %constant.147.clone.pool) | copy-start | bytes 196612
  7.2 48.5 %all-gather.6.cloned.1.call-start = ((), (), s32[]{:S(2)}) async-start(), calls=%async_computation | async-start | bytes 2703360 | tf_op jit(solution)/shard_map/all_gather | solution.py:223
  10.8 7.6 %collective-permute-start = (bf16[8,16,512]{2,1,0:T(8,128)(2,1)S(1)}, bf16[8,16,512]{2,1,0:T(8,128)(2,1)S(1)}, u32[]{:S(2)}, u32[]{:S(2)}) collective-permute-start(bf16[8,16,512]{2,1,0:T(8,128)(2,1)S(1)} %get-tuple-element.27), channel_id=1, source_target_pairs={{0,4},{4,8},{8,12},{12,16},{16,20},{20,24},{24,28},{1,5},{5,9},{9,... | collective-permute-start | bytes 393224 | tf_op jit(solution)/shard_map/ppermute | solution.py:20
  15.6 6.9 %collective-permute-start.1 = (bf16[8,16,512]{2,1,0:T(8,128)(2,1)S(1)}, bf16[8,16,512]{2,1,0:T(8,128)(2,1)S(1)}, u32[]{:S(2)}, u32[]{:S(2)}) collective-permute-start(bf16[8,16,512]{2,1,0:T(8,128)(2,1)S(1)} %get-tuple-element.26), channel_id=1, source_target_pairs={{4,0},{8,4},{12,8},{16,12},{20,16},{24,20},{28,24},{5,1},{9,5},{13... | collective-permute-start | bytes 393224 | tf_op jit(solution)/shard_map/ppermute | solution.py:20
  22.5 0.8 copy-start.3
  23.4 66.8 %all-gather.10.cloned.1.call-start = ((), (), s32[]{:S(2)}) async-start(), calls=%async_computation.2 | async-start | bytes 1179648 | tf_op jit(solution)/shard_map/all_gather | solution.py:228
  30.4 110.6 %all-gather.8.cloned.1.call-start = ((), (), s32[]{:S(2)}) async-start(), calls=%async_computation.1 | async-start | bytes 2359296 | tf_op jit(solution)/shard_map/all_gather | solution.py:265
  55.6 1.6 copy-start
  71.7 1.6 copy-start.1
  199.5 0.6 copy-start.5
  199.6 0.6 copy-start.4
Sparse Core Ops, SparseCore 0:
  23.5 24.1 all-gather.5
  49.8 40.3 all-gather.9
  92.9 48.0 all-gather.7

commit v2 on v1

--- a/solution.py
+++ b/solution.py
@@ -23,16 +23,18 @@
 def octant_maps():
     z, y, x = np.meshgrid(*[np.arange(EDGE)] * 3, indexing="ij")
     spread = np.zeros((8, CELLS, CELLS), np.float32)
-    pool = np.zeros((CELLS, 64), np.float32)
-    place = np.zeros((8, 64, CELLS), np.float32)
+    pool = np.zeros((2, CELLS, 128), np.float32)
+    place = np.zeros((2, 8, 128, CELLS), np.float32)
     fine = np.arange(CELLS)
     small = ((z // 2) * 16 + (y // 2) * 4 + x // 2).reshape(-1)
-    pool[fine, small] = 1.0
+    for half in range(2):
+        pool[half, fine, small + 64 * half] = 1.0
     for q in range(8):
         cz, cy, cx = z // 2 + 4 * (q // 4), y // 2 + 4 * (q // 2 % 2), x // 2 + 4 * (q % 2)
         coarse = (cz * 64 + cy * 8 + cx).reshape(-1)
         spread[q, coarse, fine] = 1.0
-        place[q, small, coarse] = 1.0
+        for half in range(2):
+            place[half, q, small + 64 * half, coarse] = 1.0
     return spread, pool, place
 
 
@@ -80,8 +82,11 @@
         @pl.when(jnp.logical_and(j >= 4, j < 20))
         def _():
             hidden = (v * s).astype(BF16)
-            small = jnp.dot(hidden, pool[...], preferred_element_type=F32) * 0.125
-            octants[j - 4] = small.astype(BF16)
+            half = j % 2
+            small = jnp.dot(hidden, pool[half], preferred_element_type=F32) * 0.125
+            pair = (j - 4) // 2
+            kept = jnp.where(half == 0, 0.0, octants[pair].astype(F32))
+            octants[pair] = (kept + small).astype(BF16)
 
         return carry
 
@@ -95,7 +100,7 @@
     views, coarse_in, coarse_act, coarse_delta, coarse_back, fine_delta, bias_sum,
 ):
     width = table.shape[1]
-    group = fine_grad.shape[1]
+    slots, group = fine_grad.shape[0], fine_grad.shape[1]
     chan, live, parent0, coarse_row, coarse_live = (facts[n] for n in range(5))
     mine = pl.ds(pl.multiple_of(chan * group, group), group)
 
@@ -108,9 +113,12 @@
     def assemble(k, carry):
         total = jnp.zeros((width, CELLS), F32)
         for q in range(8):
-            total += jnp.dot(
-                octants[octant_at[k * 8 + q]], place[q], preferred_element_type=F32
+            at = octant_at[k * 8 + q]
+            owner, slot = at // slots, at % slots
+            both = jnp.concatenate(
+                [octants[c, owner, slot // 2] for c in range(octants.shape[0])], axis=0
             )
+            total += jnp.dot(both, place[slot % 2, q], preferred_element_type=F32)
         inside = jnp.logical_and(k >= facts[5], k < facts[6])
         coarse_in[k] = jnp.where(inside, total, 0.0).astype(BF16)
         return carry
@@ -195,6 +203,106 @@
 
     lax.fori_loop(0, fine_grad.shape[0], fine_row, 0)
     fine_bg[...] = jnp.broadcast_to(jnp.sum(bias_sum[...], axis=1, keepdims=True), fine_bg.shape)
+
+
+def greet(axis):
+    size, me = lax.axis_size(axis), lax.axis_index(axis)
+    barrier = pltpu.get_barrier_semaphore()
+
+    def one(d, carry):
+        pl.semaphore_signal(
+            barrier, inc=1, device_id={axis: (me + d) % size}, device_id_type=pl.DeviceIdType.MESH
+        )
+        return carry
+
+    lax.fori_loop(1, size, one, 0)
+    return size - 1
+
+
+def push(src, dst, send_sem, recv_sem, axis, peer):
+    return pltpu.make_async_remote_copy(
+        src_ref=src,
+        dst_ref=dst,
+        send_sem=send_sem,
+        recv_sem=recv_sem,
+        device_id={axis: peer},
+        device_id_type=pl.DeviceIdType.MESH,
+    )
+
+
+def exchange(axis, source, target, send_sem, recv_sem):
+    size, me = lax.axis_size(axis), lax.axis_index(axis)
+
+    def start(d, carry):
+        peer = (me + d) % size
+        push(source(peer), target(me, d), send_sem.at[d], recv_sem.at[d], axis, peer).start()
+        return carry
+
+    def finish(d, carry):
+        peer = (me + d) % size
+        giver = (me + size - d) % size
+        push(source(peer), target(me, d), send_sem.at[d], recv_sem.at[d], axis, peer).wait_send()
+        push(source(peer), target(giver, d), send_sem.at[d], recv_sem.at[d], axis, peer).wait_recv()
+        return carry
+
+    lax.fori_loop(1, size, start, 0)
+    lax.fori_loop(1, size, finish, 0)
+
+
+def octant_kernel(octants, out, send_b, recv_b, send_c, recv_c, own_sem):
+    me, chan = lax.axis_index("blocks"), lax.axis_index("chan")
+    group = out.shape[3]
+    pl.semaphore_wait(pltpu.get_barrier_semaphore(), greet("blocks") + greet("chan"))
+    mine = octants.at[:, pl.ds(pl.multiple_of(chan * group, group), group), :]
+    kept = pltpu.make_async_copy(mine, out.at[chan, me], own_sem)
+    kept.start()
+    exchange("blocks", lambda p: mine, lambda p, d: out.at[chan, p], send_b, recv_b)
+    kept.wait()
+    exchange("chan", lambda p: out.at[chan], lambda p, d: out.at[p], send_c, recv_c)
+
+
+def share_octants(octants, group):
+    n, width = lax.axis_size("blocks"), lax.axis_size("chan")
+    return pl.pallas_call(
+        octant_kernel,
+        out_shape=jax.ShapeDtypeStruct((width, n, octants.shape[0], group, 128), BF16),
+        in_specs=[pl.BlockSpec(memory_space=pltpu.VMEM)],
+        out_specs=pl.BlockSpec(memory_space=pltpu.VMEM),
+        scratch_shapes=[
+            pltpu.SemaphoreType.DMA((n,)),
+            pltpu.SemaphoreType.DMA((n,)),
+            pltpu.SemaphoreType.DMA((width,)),
+            pltpu.SemaphoreType.DMA((width,)),
+            pltpu.SemaphoreType.DMA,
+        ],
+        compiler_params=pltpu.CompilerParams(
+            collective_id=1, has_side_effects=True, vmem_limit_bytes=32 * 2**20
+        ),
+    )(octants)
+
+
+def sum_kernel(part, out, landed, send_a, recv_a, send_b, recv_b):
+    me = lax.axis_index("blocks")
+    size = part.shape[0]
+    pl.semaphore_wait(pltpu.get_barrier_semaphore(), greet("blocks"))
+    exchange("blocks", lambda p: part.at[p], lambda p, d: landed.at[d], send_a, recv_a)
+    out[me] = lax.fori_loop(1, size, lambda d, total: total + landed[d], part[me])
+    exchange("blocks", lambda p: out.at[me], lambda p, d: out.at[p], send_b, recv_b)
+
+
+def sum_over_blocks(partial):
+    n = lax.axis_size("blocks")
+    rows, width = partial.shape
+    shape = (n, rows // n, width)
+    summed = pl.pallas_call(
+        sum_kernel,
+        out_shape=jax.ShapeDtypeStruct(shape, F32),
+        in_specs=[pl.BlockSpec(memory_space=pltpu.VMEM)],
+        out_specs=pl.BlockSpec(memory_space=pltpu.VMEM),
+        scratch_shapes=[pltpu.VMEM(shape, F32)] + [pltpu.SemaphoreType.DMA((n,))] * 4,
+        compiler_params=pltpu.CompilerParams(collective_id=2, has_side_effects=True),
+    )(partial.reshape(shape))
+    return summed.reshape(rows, width)
 
 
 def local(
@@ -248,7 +356,7 @@
         forward_kernel,
         out_shape=(
             jax.ShapeDtypeStruct((delta_rows, channels, cells), F32),
-            jax.ShapeDtypeStruct((slots, channels, 64), BF16),
+            jax.ShapeDtypeStruct((slots // 2, channels, 128), BF16),
         ),
         in_specs=[smem] + [vmem] * 4,
         out_specs=(vmem, vmem),
@@ -262,7 +370,7 @@
         pool,
     )
 
-    every_octant = lax.all_gather(octants, "blocks", axis=0, tiled=True)
+    every_octant = share_octants(octants, group)
     parent = (first - 4) // 8
 
     def owner_of(block):
@@ -334,7 +442,7 @@
         spread,
     )
     partial = jnp.concatenate([fine_wg, fine_bg, coarse_wg, coarse_bg], axis=0)
-    sums = jnp.sum(lax.all_gather(partial, "blocks", axis=0), axis=0)
+    sums = sum_over_blocks(partial)
     half = 8 * group
     fine_norm = jnp.sqrt(total.astype(F32) * cells)
     coarse_norm = jnp.sqrt(coarse_total.astype(F32) * cells)

time: 207 us -> 155 us (0.75)
  waiting for transfers between devices: 66.5 us -> 3.79 us
  Pallas kernels: 37.3 us -> 78.3 us
  blocking collectives: 51 us -> 17.7 us
    all_gather x1 -> x0, waiting for transfers between devices: 50.8 us -> none  [local(): every_octant = lax.all_gather(octants, 'blocks', axis=0, tiled=True)]
    pallas_call x0 -> x2, Pallas kernels: none -> 42.5 us  [the longest x1 23.8 us: share_octants(): pl.pallas_call(octant_kernel, out_shape=jax.ShapeDtypeStruct((width, n, o...]
    all_gather x1 -> x0, blocking collectives: 33.3 us -> none  [local(): sums = jnp.sum(lax.all_gather(partial, 'blocks', axis=0), axis=0)]
    all_gather x1, waiting for transfers between devices: 11.8 us -> 0.01 us  [local(): lax.all_gather(lax.all_gather(coarse_cotangent, 'chan', axis=1, tiled=Tru...]
    unnamed x32 -> x34, local copies, waits for them, and re-layouts: 5.59 us -> 6.51 us
  transfers between devices with their start and end apart: 5 -> 4, of which waited for: 4 -> 2; matrix products, arithmetic and copies ran while one was open for 7% -> 9% of each run, Pallas kernels for 7% -> 24%
where the time goes in v2:
time: 155 us; the launch traced here: 154 us
  Pallas kernels  78.3 us (51%)
  between operations  23 us (15%)
  blocking collectives  17.7 us (11%)
  local copies, waits for them, and re-layouts  15.6 us (10%)
  other arithmetic  9.83 us (6%)
  starting transfers between devices  6.21 us (4%)
  waiting for transfers between devices  3.79 us (2%)
    pallas_call x1, Pallas kernels, share_octants(): pl.pallas_call(octant_kernel, out_shape=jax.ShapeDtypeStruct((width, n, o...  23.8 us
    pallas_call x1, Pallas kernels, local(): pl.pallas_call(backward_kernel, out_shape=(jax.ShapeDtypeStruct((coarse_s...  22 us
    pallas_call x1, Pallas kernels, sum_over_blocks(): pl.pallas_call(sum_kernel, out_shape=jax.ShapeDtypeStruct(shape, F32), in...  18.6 us
    pallas_call x1, Pallas kernels, local(): pl.pallas_call(forward_kernel, out_shape=(jax.ShapeDtypeStruct((delta_row...  13.8 us
    all_gather x1, blocking collectives, local(): lax.all_gather(coarse_cotangent, 'chan', axis=1, tiled=True)  6.96 us
    unnamed x34, local copies, waits for them, and re-layouts  6.51 us
    ppermute x2, starting transfers between devices, from_behind(): return lax.ppermute(block, axis, route)  6.13 us
    all_gather x1, blocking collectives, local(): lax.all_gather(jnp.concatenate([fine_weight, coarse_weight]), 'chan', axi...  5.7 us
  transfers between devices with their start and end apart: 4, of which 2 were waited for; matrix products, arithmetic and copies ran while one was open for 9% of the time, Pallas kernels for 24%

profile of v2, /device:TPU:0, one launch (start us, length us, event | category | flops | bytes accessed | tf_op | source)
XLA Modules:
  0.0 154.4 jit_solution(14010365315433254138)
XLA Ops:
  7.2 1.3 dynamic_slice.13
  9.8 1.0 fusion.8
  10.8 4.8 %collective-permute-start = (bf16[8,16,512]{2,1,0:T(8,128)(2,1)S(1)}, bf16[8,16,512]{2,1,0:T(8,128)(2,1)S(1)}, u32[]{:S(2)}, u32[]{:S(2)}) collective-permute-start(bf16[8,16,512]{2,1,0:T(8,128)(2,1)S(1)} %get-tuple-element.27), channel_id=1, source_target_pairs={{0,4},{4,8},{8,12},{12,16},{16,20},{20,24},{24,28},{1,5},{5,9},{9,... | collective-permute-start | bytes 393224 | tf_op jit(solution)/shard_map/ppermute | solution.py:20
  15.7 1.3 collective-permute-start.1
  17.7 0.7 collective-permute-done
  18.4 1.1 maximum_maximum_fusion
  19.4 3.1 %collective-permute-done.1 = bf16[8,16,512]{2,1,0:T(8,128)(2,1)S(1)} collective-permute-done((bf16[8,16,512]{2,1,0:T(8,128)(2,1)S(1)}, bf16[8,16,512]{2,1,0:T(8,128)(2,1)S(1)}, u32[]{:S(2)}, u32[]{:S(2)}) %collective-permute-start.1) | collective-permute-done | bytes 131104 | tf_op jit(solution)/shard_map/ppermute | solution.py:20
  22.5 0.8 copy-done.4
  23.4 7.0 %all_gather.18 = bf16[2,64,512]{2,1,0:T(8,128)(2,1)} all-gather(bf16[2,16,512]{2,1,0:T(8,128)(2,1)} %param.17), channel_id=1, replica_groups=mesh['blocks'=8,'chan'=4] {'chan'}, dimensions={1}, use_global_device_ids=true | all-gather | bytes 163840 | tf_op jit(solution)/shard_map/all_gather | solution.py:337
  30.4 1.3 reduce_sum.37
  35.6 0.8 select_reduce_fusion
  36.4 0.6 dynamic_slice.12
  39.6 0.7 add_compare_fusion
  40.5 0.7 maximum_bitcast_fusion
  41.1 5.1 %all-gather = f32[4,16,2]{1,2,0:T(2,128)S(1)} all-gather(f32[1,16,2]{1,2,0:T(2,128)S(1)} %maximum_bitcast_fusion), channel_id=1, replica_groups=mesh['blocks'=8,'chan'=4] {'chan'}, dimensions={0}, use_global_device_ids=true | all-gather | bytes 640 | tf_op jit(solution)/shard_map/all_gather | solution.py:335
  46.2 0.1 reshape.228
  46.3 0.7 add_select_fusion
  47.1 0.1 copy.40
  47.2 0.6 reshape.221.near
  47.8 0.1 copy.41
  47.9 0.1 select_n.119.near
  48.0 0.7 copy.48.coarse_b
  48.7 0.1 copy.44.bias
  48.8 0.8 pad_maximum_fusion.1
  49.6 5.7 %all_gather.16 = bf16[14,64,64]{2,1,0:T(8,128)(2,1)S(1)} all-gather(bf16[14,16,64]{2,1,0:T(8,128)(2,1)S(1)} %pad_maximum_fusion.1), channel_id=1, replica_groups=mesh['blocks'=8,'chan'=4] {'chan'}, dimensions={1}, use_global_device_ids=true | all-gather | bytes 143360 | tf_op jit(solution)/shard_map/all_gather | solution.py:332
  55.4 0.1 constant_dynamic-slice_fusion.1
  55.5 0.7 copy.51.back_w
  56.2 0.7 copy.49.back_coarse_w
  56.9 0.1 copy.45
  57.0 0.8 reshape.223.forward_w
  57.8 0.1 reshape.222.weight
  58.0 1.2 stack.58.facts
  59.2 0.2 fusion.2
  59.4 0.1 fusion
  59.5 0.6 fusion.6.cotangent_at
  60.1 0.5 add_subtract_fusion.octant_at
  60.6 1.6 %copy-done = bf16[33,64,512]{2,1,0:T(8,128)(2,1)S(1)} copy-done((bf16[33,64,512]{2,1,0:T(8,128)(2,1)S(1)}, bf16[33,64,512]{2,1,0:T(8,128)(2,1)}, u32[]{:S(2)}) %copy-start) | copy-done | bytes 2162712
  62.2 13.8 %shard_map.154 = (f32[24,64,512]{2,1,0:T(8,128)S(1)}, bf16[8,64,128]{2,1,0:T(8,128)(2,1)S(1)}) custom-call(s32[144]{0:T(256)S(1)} %select_n.119.near, bf16[33,64,512]{2,1,0:T(8,128)(2,1)S(1)} %copy-done, bf16[64,448]{1,0:T(8,128)(2,1)S(1)} %reshape.222.weight, f32[64,1]{1,0:T(8,128)S(1)} %copy.44.bias, bf16[2,512,128]{2,1,0:T(8,128)(2,1)S(1)} %copy-done.3), custom_call_target="tpu_custom_call" | custom-call | tf_op jit(solution)/shard_map/pallas_call | solution.py:355
  76.0 1.6 %copy-done.2 = f32[24,64,512]{2,1,0:T(8,128)} copy-done((f32[24,64,512]{2,1,0:T(8,128)}, f32[24,64,512]{2,1,0:T(8,128)S(1)}, u32[]{:S(2)}) %copy-start.2) | copy-done | bytes 3145752
  77.7 23.8 %shard_map.155.octants = bf16[4,8,8,16,128]{4,3,2,1,0:T(8,128)(2,1)S(1)} custom-call(bf16[8,64,128]{2,1,0:T(8,128)(2,1)S(1)} %get-tuple-element.15.octants), custom_call_target="tpu_custom_call" | custom-call | tf_op jit(solution)/shard_map/pallas_call | solution.py:266
  101.5 1.0 copy-done.1
  102.5 22.0 %shard_map.156 = (bf16[2,16,512]{2,1,0:T(8,128)(2,1)}, bf16[16,16,512]{2,1,0:T(8,128)(2,1)}, f32[112,64]{1,0:T(8,128)}, f32[16,64]{1,0:T(8,128)}, f32[112,64]{1,0:T(8,128)}, /*index=5*/f32[16,64]{1,0:T(8,128)}) custom-call(s32[96]{0:T(128)} %reshape.221.near, s32[7]{0:T(128)} %stack.58.facts, s32[64]{0:T(128)} %add_subtract_fusion.octant_at, ...), custom_call_target="tpu_custom_call" | custom-call | tf_op jit(solution)/shard_map/pallas_call | solution.py:406
  124.5 1.5 pad_maximum_fusion
  126.0 18.6 %shard_map.157 = f32[8,32,64]{2,1,0:T(8,128)} custom-call(f32[8,32,64]{2,1,0:T(8,128)} %bitcast.94), custom_call_target="tpu_custom_call" | custom-call | tf_op jit(solution)/shard_map/pallas_call | solution.py:297
  144.7 0.9 slice_divide_fusion
  145.6 0.6 slice_reduce_fusion.1
  146.2 0.6 slice_reduce_fusion
  146.9 0.5 copy-done.6
  (49 shorter events, 0.7 us)
Async XLA Ops:
  7.2 53.4 %copy-start.3 = (bf16[2,512,128]{2,1,0:T(8,128)(2,1)S(1)}, bf16[2,512,128]{2,1,0:T(8,128)(2,1)}, u32[]{:S(2)}) copy-start(bf16[2,512,128]{2,1,0:T(8,128)(2,1)} %constant.145.clone.pool) | copy-start | bytes 786436
  7.2 53.4 %all-gather.4.cloned.1.call-start = ((), (), s32[]{:S(2)}) async-start(), calls=%async_computation | async-start | bytes 2703360 | tf_op jit(solution)/shard_map/all_gather | solution.py:331
  10.8 7.6 %collective-permute-start = (bf16[8,16,512]{2,1,0:T(8,128)(2,1)S(1)}, bf16[8,16,512]{2,1,0:T(8,128)(2,1)S(1)}, u32[]{:S(2)}, u32[]{:S(2)}) collective-permute-start(bf16[8,16,512]{2,1,0:T(8,128)(2,1)S(1)} %get-tuple-element.27), channel_id=1, source_target_pairs={{0,4},{4,8},{8,12},{12,16},{16,20},{20,24},{24,28},{1,5},{5,9},{9,... | collective-permute-start | bytes 393224 | tf_op jit(solution)/shard_map/ppermute | solution.py:20
  15.7 6.9 %collective-permute-start.1 = (bf16[8,16,512]{2,1,0:T(8,128)(2,1)S(1)}, bf16[8,16,512]{2,1,0:T(8,128)(2,1)S(1)}, u32[]{:S(2)}, u32[]{:S(2)}) collective-permute-start(bf16[8,16,512]{2,1,0:T(8,128)(2,1)S(1)} %get-tuple-element.26), channel_id=1, source_target_pairs={{4,0},{8,4},{12,8},{16,12},{20,16},{24,20},{28,24},{5,1},{9,5},{13... | collective-permute-start | bytes 393224 | tf_op jit(solution)/shard_map/ppermute | solution.py:20
  22.5 0.8 copy-start.4
  23.4 79.2 %all-gather.6.cloned.1.call-start = ((), (), s32[]{:S(2)}) async-start(), calls=%async_computation.1 | async-start | bytes 1179648 | tf_op jit(solution)/shard_map/all_gather | solution.py:336
  60.6 1.6 %copy-start = (bf16[33,64,512]{2,1,0:T(8,128)(2,1)S(1)}, bf16[33,64,512]{2,1,0:T(8,128)(2,1)}, u32[]{:S(2)}) copy-start(bf16[33,64,512]{2,1,0:T(8,128)(2,1)} %all-gather.4.cloned.1.call-done.table) | copy-start | bytes 6488068
  76.0 1.6 %copy-start.2 = (f32[24,64,512]{2,1,0:T(8,128)}, f32[24,64,512]{2,1,0:T(8,128)S(1)}, u32[]{:S(2)}) copy-start(f32[24,64,512]{2,1,0:T(8,128)S(1)} %get-tuple-element.14.slope) | copy-start | bytes 9437188
  101.5 1.0 copy-start.1
  146.9 0.6 copy-start.6
  146.9 0.6 copy-start.5
Sparse Core Ops, SparseCore 0:
  23.5 24.1 all-gather.3
  49.8 43.6 all-gather.5

commit v3 on v2

--- a/solution.py
+++ b/solution.py
@@ -12,12 +12,6 @@
 STRIDES = (1, 8, 64)
 F32 = jnp.float32
 BF16 = jnp.bfloat16
-
-
-def from_behind(block, axis, distance):
-    devices = range(lax.axis_size(axis))
-    route = [(i - distance, i) for i in devices if i - distance in devices]
-    return lax.ppermute(block, axis, route)
 
 
 def octant_maps():
@@ -73,8 +67,8 @@
     width = table.shape[1]
 
     def row(j, carry):
-        own = table[j + 4]
-        write_views(views, own, [table[near[j * 6 + n]] for n in range(6)], width)
+        own = table[near[j * 7 + 6]]
+        write_views(views, own, [table[near[j * 7 + n]] for n in range(6)], width)
         v = jnp.dot(weight[...], views[...], preferred_element_type=F32) + bias[...]
         s = sigmoid(v)
         slope[j] = s * (1.0 + v * (1.0 - s))
@@ -249,16 +243,147 @@
     lax.fori_loop(1, size, finish, 0)
 
 
+def chan_peers():
+    me = lax.axis_index("chan")
+    size = lax.axis_size("chan")
+    far, near = (me + size // 2) % size, me + 1 - 2 * (me % 2)
+    return me, far, near, (near + size // 2) % size
+
+
+def greet_chan():
+    _, far, near, _ = chan_peers()
+    for peer in (far, near):
+        pl.semaphore_signal(
+            pltpu.get_barrier_semaphore(),
+            inc=1,
+            device_id={"chan": peer},
+            device_id_type=pl.DeviceIdType.MESH,
+        )
+    return 2
+
+
+def share_chan(parts, send_sem, recv_sem, base):
+    me, far, near, near_far = chan_peers()
+
+    def copy(n, k, held, peer):
+        place = parts[n](held)
+        at = base + 3 * n + k
+        return push(place, place, send_sem.at[at], recv_sem.at[at], "chan", peer)
+
+    def first():
+        for n in range(len(parts)):
+            copy(n, 0, me, far).start()
+            copy(n, 1, me, near).start()
+
+    def second():
+        for n in range(len(parts)):
+            copy(n, 0, far, far).wait_recv()
+            copy(n, 2, far, near).start()
+        return third
+
+    def third():
+        for n in range(len(parts)):
+            copy(n, 1, near, near).wait_recv()
+            copy(n, 2, near_far, near).wait_recv()
+            copy(n, 0, me, far).wait_send()
+            copy(n, 1, me, near).wait_send()
+            copy(n, 2, far, near).wait_send()
+
+    return first, second
+
+
+def gather_kernel(
+    tail, own, weight, bias, cotangent, table, weights, biases, cotangents,
+    send_b, recv_b, send_c, recv_c,
+):
+    me, n = lax.axis_index("blocks"), lax.axis_size("blocks")
+    chan = lax.axis_index("chan")
+    slots, group, cells = own.shape
+    after, before = (me + 1) % n, (me + n - 1) % n
+    for peer in (after, before):
+        pl.semaphore_signal(
+            pltpu.get_barrier_semaphore(),
+            inc=1,
+            device_id={"blocks": peer},
+            device_id_type=pl.DeviceIdType.MESH,
+        )
+    pl.semaphore_wait(pltpu.get_barrier_semaphore(), greet_chan() + 2)
+
+    def lane(c):
+        return pl.ds(pl.multiple_of(c * group, group), group)
+
+    def rows(first, count):
+        return lambda c: table.at[pl.ds(first, count), lane(c), :]
+
+    lower, upper = rows(0, 8), rows(8 + slots, 8)
+    down = push(own.at[pl.ds(0, 8)], upper(chan), send_b.at[0], recv_b.at[0], "blocks", before)
+    up = push(tail, lower(chan), send_b.at[1], recv_b.at[1], "blocks", after)
+    down.start()
+    up.start()
+    table[8 : 8 + slots, lane(chan), :] = own[...]
+    weights[:, lane(chan), :] = weight[...]
+    biases[chan] = bias[...]
+    cotangents[:, lane(chan), :] = cotangent[...]
+    table[16 + slots] = jnp.zeros(table.shape[1:], BF16)
+    first, second = share_chan(
+        [
+            rows(8, slots),
+            lambda c: weights.at[:, lane(c), :],
+            lambda c: biases.at[c],
+            lambda c: cotangents.at[:, lane(c), :],
+        ],
+        send_c, recv_c, 0,
+    )
+    halo_first, halo_second = share_chan([lower, upper], send_c, recv_c, 12)
+    first()
+    down.wait()
+    up.wait()
+    halo_first()
+    third = second()
+    halo_third = halo_second()
+    third()
+    halo_third()
+
+
+def gather_start(tail, own, weight, bias, cotangent):
+    width = lax.axis_size("chan")
+    slots, group, cells = own.shape
+    channels = group * width
+    vmem = pl.BlockSpec(memory_space=pltpu.VMEM)
+    return pl.pallas_call(
+        gather_kernel,
+        out_shape=(
+            jax.ShapeDtypeStruct((slots + 17, channels, cells), BF16),
+            jax.ShapeDtypeStruct((weight.shape[0], channels, channels), BF16),
+            jax.ShapeDtypeStruct((width,) + bias.shape, F32),
+            jax.ShapeDtypeStruct((cotangent.shape[0], channels, cells), BF16),
+        ),
+        in_specs=[vmem] * 5,
+        out_specs=(vmem,) * 4,
+        scratch_shapes=[
+            pltpu.SemaphoreType.DMA((2,)),
+            pltpu.SemaphoreType.DMA((2,)),
+            pltpu.SemaphoreType.DMA((18,)),
+            pltpu.SemaphoreType.DMA((18,)),
+        ],
+        compiler_params=pltpu.CompilerParams(
+            collective_id=3, has_side_effects=True, vmem_limit_bytes=32 * 2**20
+        ),
+    )(tail, own, weight, bias, cotangent)
+
+
 def octant_kernel(octants, out, send_b, recv_b, send_c, recv_c, own_sem):
     me, chan = lax.axis_index("blocks"), lax.axis_index("chan")
     group = out.shape[3]
-    pl.semaphore_wait(pltpu.get_barrier_semaphore(), greet("blocks") + greet("chan"))
+    pl.semaphore_wait(pltpu.get_barrier_semaphore(), greet("blocks") + greet_chan())
     mine = octants.at[:, pl.ds(pl.multiple_of(chan * group, group), group), :]
     kept = pltpu.make_async_copy(mine, out.at[chan, me], own_sem)
     kept.start()
     exchange("blocks", lambda p: mine, lambda p, d: out.at[chan, p], send_b, recv_b)
     kept.wait()
-    exchange("chan", lambda p: out.at[chan], lambda p, d: out.at[p], send_c, recv_c)
+    first, second = share_chan([lambda c: out.at[c]], send_c, recv_c, 0)
+    first()
+    second()()
 
 
 def share_octants(octants, group):
@@ -271,8 +396,8 @@
         scratch_shapes=[
             pltpu.SemaphoreType.DMA((n,)),
             pltpu.SemaphoreType.DMA((n,)),
-            pltpu.SemaphoreType.DMA((width,)),
-            pltpu.SemaphoreType.DMA((width,)),
+            pltpu.SemaphoreType.DMA((3,)),
+            pltpu.SemaphoreType.DMA((3,)),
             pltpu.SemaphoreType.DMA,
         ],
         compiler_params=pltpu.CompilerParams(
@@ -323,19 +448,17 @@
     coarse_first = (first + 7) // 8
     coarse_count = (first + live + 7) // 8 - coarse_first
 
-    lower = from_behind(lax.dynamic_slice_in_dim(fine_input, live - 8, 8, 0), "blocks", 1)
-    upper = from_behind(fine_input[:8], "blocks", -1)
     rows = slots + 16
-    table = jnp.concatenate([lower, fine_input, jnp.zeros((9, group, cells), BF16)], axis=0)
-    table = lax.dynamic_update_slice_in_dim(table, upper, 8 + live, 0)
-    table = lax.all_gather(table, "chan", axis=1, tiled=True)
-    weights = lax.all_gather(
-        jnp.concatenate([fine_weight, coarse_weight]), "chan", axis=1, tiled=True
-    )
-    biases = lax.all_gather(jnp.stack([fine_bias, coarse_bias]), "chan", axis=1, tiled=True)
-    cotangents = lax.all_gather(
-        lax.all_gather(coarse_cotangent, "chan", axis=1, tiled=True), "blocks", axis=0, tiled=True
-    )
+    tail = lax.dynamic_slice_in_dim(fine_input, live - 8, 8, 0)
+    table, weights, biases, cotangents = gather_start(
+        tail,
+        fine_input,
+        jnp.concatenate([fine_weight, coarse_weight]),
+        jnp.stack([fine_bias, coarse_bias]),
+        coarse_cotangent,
+    )
+    biases = biases.transpose(1, 0, 2).reshape(2, channels)
+    cotangents = lax.all_gather(cotangents, "blocks", axis=0, tiled=True)
     full_fine, full_coarse = weights[:7], weights[7:]
 
     spread, pool, place = (jnp.asarray(a, BF16) for a in octant_maps())
@@ -347,7 +470,13 @@
     )
     offsets = jnp.array([-1, 1, -2, 2, -4, 4], jnp.int32)[None, :]
     spot = jnp.arange(delta_rows, dtype=jnp.int32)[:, None] + offsets
-    near_fine = jnp.where(valid, spot + 4, rows).reshape(-1)
+
+    def table_row(r):
+        return jnp.where(r < 8 + live, r, jnp.minimum(r + slots - live, rows - 1))
+
+    own_row = table_row(jnp.arange(delta_rows, dtype=jnp.int32) + 4)
+    near_fine = jnp.where(valid, table_row(spot + 4), rows)
+    near_fine = jnp.concatenate([near_fine, own_row[:, None]], axis=1).reshape(-1)
     near_delta = jnp.where(valid, spot, delta_rows)[4 : 4 + slots].reshape(-1)
 
     smem = pl.BlockSpec(memory_space=pltpu.SMEM)

time: 155 us -> 141 us (0.910)
  blocking collectives: 17.7 us -> 0 us
  Pallas kernels: 78.3 us -> 93.8 us
  starting transfers between devices: 6.21 us -> 0.04 us
  waiting for transfers between devices: 3.79 us -> 0.02 us
    pallas_call x0 -> x1, Pallas kernels: none -> 23.1 us  [gather_start(): pl.pallas_call(gather_kernel, out_shape=(jax.ShapeDtypeStruct((slots + 17...]
    all_gather x3 -> x0, blocking collectives: 17.7 us -> none  [the longest x1 6.96 us: local(): lax.all_gather(coarse_cotangent, 'chan', axis=1, tiled=True)]
    pallas_call x1, Pallas kernels: 23.8 us -> 15.6 us  [share_octants(): pl.pallas_call(octant_kernel, out_shape=jax.ShapeDtypeStruct((width, n, o...]
    ppermute x2 -> x0, starting transfers between devices: 6.13 us -> none  [from_behind(): return lax.ppermute(block, axis, route)]
    ppermute x2 -> x0, waiting for transfers between devices: 3.76 us -> none  [from_behind(): return lax.ppermute(block, axis, route)]
    unnamed x34 -> x35, local copies, waits for them, and re-layouts: 6.51 us -> 5.75 us
  transfers between devices with their start and end apart: 4 -> 1, of which waited for: 2 -> 0; matrix products, arithmetic and copies ran while one was open for 9% -> 9% of each run, Pallas kernels for 24% -> 21%
where the time goes in v3:
time: 141 us
  Pallas kernels  93.8 us (67%)
  between operations  22.3 us (16%)
  local copies, waits for them, and re-layouts  14.8 us (10%)
  other arithmetic  10.1 us (7%)
    pallas_call x1, Pallas kernels, local(): pl.pallas_call(backward_kernel, out_shape=(jax.ShapeDtypeStruct((coarse_s...  23.3 us
    pallas_call x1, Pallas kernels, gather_start(): pl.pallas_call(gather_kernel, out_shape=(jax.ShapeDtypeStruct((slots + 17...  23.1 us
    pallas_call x1, Pallas kernels, sum_over_blocks(): pl.pallas_call(sum_kernel, out_shape=jax.ShapeDtypeStruct(shape, F32), in...  17.9 us
    pallas_call x1, Pallas kernels, share_octants(): pl.pallas_call(octant_kernel, out_shape=jax.ShapeDtypeStruct((width, n, o...  15.6 us
    pallas_call x1, Pallas kernels, local(): pl.pallas_call(forward_kernel, out_shape=(jax.ShapeDtypeStruct((delta_row...  13.8 us
    unnamed x35, local copies, waits for them, and re-layouts  5.75 us
  transfers between devices with their start and end apart: 1, of which 0 were waited for; matrix products, arithmetic and copies ran while one was open for 9% of the time, Pallas kernels for 21%

profile of v3, /device:TPU:0, one launch (start us, length us, event | category | flops | bytes accessed | tf_op | source)
XLA Modules:
  0.0 141.0 jit_solution(10822938947388781131)
XLA Ops:
  7.2 0.0 copy-start.4
  7.2 0.0 all-gather.2.cloned.1.call-start
  7.2 1.3 dynamic_slice.13
  9.8 0.7 pad_maximum_fusion.2.bias
  10.5 0.8 pad_maximum_fusion.1.weight
  11.3 0.9 constant_dynamic-slice_fusion.1.tail
  12.2 0.0 copy-start.3
  12.2 0.9 copy-done.3
  13.1 0.8 copy-done.5
  13.9 23.1 %shard_map.154 = (bf16[33,64,512]{2,1,0:T(8,128)(2,1)S(1)}, bf16[14,64,64]{2,1,0:T(8,128)(2,1)S(1)}, f32[4,2,16]{2,1,0:T(2,128)S(1)}, bf16[2,64,512]{2,1,0:T(8,128)(2,1)}) custom-call(bf16[8,16,512]{2,1,0:T(8,128)(2,1)S(1)} %constant_dynamic-slice_fusion.1.tail, bf16[16,16,512]{2,1,0:T(8,128)(2,1)S(1)} %copy-done.3, ...), custom_call_target="tpu_custom_call" | custom-call | tf_op jit(solution)/shard_map/pallas_call | solution.py:353
  37.0 0.0 all-gather.2.cloned.1.call-update
  37.1 1.3 reduce_sum.37
  42.3 0.8 select_reduce_fusion
  43.1 0.6 dynamic_slice.12
  46.3 0.7 compare_select_fusion.3
  46.9 0.7 add_compare_fusion
  47.8 1.4 fusion.4
  49.2 0.1 slice.187
  49.3 0.1 copy.37
  49.4 0.6 reshape.232.near
  50.0 0.1 copy.38
  50.1 0.1 reshape.233.near
  50.2 0.7 broadcast_in_dim_squeeze.9.coarse_b
  50.9 0.1 broadcast_in_dim_squeeze.8.bias
  51.1 0.1 constant_dynamic-slice_fusion
  51.2 0.7 copy.47.back_w
  51.9 0.7 copy.45.back_coarse_w
  52.6 0.1 copy.41
  52.7 0.8 reshape.235.forward_w
  53.5 0.1 copy.39
  53.6 0.1 reshape.234.weight
  53.7 13.8 %shard_map.155 = (f32[24,64,512]{2,1,0:T(8,128)S(1)}, bf16[8,64,128]{2,1,0:T(8,128)(2,1)S(1)}) custom-call(s32[168]{0:T(256)S(1)} %reshape.233.near, bf16[33,64,512]{2,1,0:T(8,128)(2,1)S(1)} %get-tuple-element.18.table, bf16[64,448]{1,0:T(8,128)(2,1)S(1)} %reshape.234.weight, f32[64,1]{1,0:T(8,128)S(1)} %broadcast_in_dim_squeeze.8.bias, ...), custom_call_target="tpu_custom_call" | custom-call | tf_op jit(solution)/shard_map/pallas_call | solution.py:484
  67.6 1.7 %copy-done.2 = f32[24,64,512]{2,1,0:T(8,128)} copy-done((f32[24,64,512]{2,1,0:T(8,128)}, f32[24,64,512]{2,1,0:T(8,128)S(1)}, u32[]{:S(2)}) %copy-start.2) | copy-done | bytes 3145752
  69.2 15.6 %shard_map.156.octants = bf16[4,8,8,16,128]{4,3,2,1,0:T(8,128)(2,1)S(1)} custom-call(bf16[8,64,128]{2,1,0:T(8,128)(2,1)S(1)} %get-tuple-element.22.octants), custom_call_target="tpu_custom_call" | custom-call | tf_op jit(solution)/shard_map/pallas_call | solution.py:391
  84.9 1.0 copy-done.1
  85.9 1.3 stack.58.facts
  87.2 0.2 fusion.2
  87.4 0.1 fusion
  87.5 0.5 fusion.7.cotangent_at
  88.0 0.5 add_subtract_fusion.octant_at
  88.5 23.3 %shard_map.157 = (bf16[2,16,512]{2,1,0:T(8,128)(2,1)}, bf16[16,16,512]{2,1,0:T(8,128)(2,1)}, f32[112,64]{1,0:T(8,128)}, f32[16,64]{1,0:T(8,128)}, f32[112,64]{1,0:T(8,128)}, /*index=5*/f32[16,64]{1,0:T(8,128)}) custom-call(s32[96]{0:T(128)} %reshape.232.near, s32[7]{0:T(128)} %stack.58.facts, s32[64]{0:T(128)} %add_subtract_fusion.octant_at, ...), custom_call_target="tpu_custom_call" | custom-call | tf_op jit(solution)/shard_map/pallas_call | solution.py:535
  111.8 1.5 %pad_maximum_fusion = f32[256,64]{1,0:T(8,128)} fusion(f32[16,64]{1,0:T(8,128)} %get-tuple-element.29, f32[112,64]{1,0:T(8,128)} %get-tuple-element.28, f32[16,64]{1,0:T(8,128)} %get-tuple-element.27, f32[112,64]{1,0:T(8,128)} %get-tuple-element.26), kind=kLoop, calls=%fused_computation | loop fusion | flops 49152 | bytes 131072 | tf_op jit(solution)/shard_map/concatenate | solution.py:573
  113.4 17.9 %shard_map.158 = f32[8,32,64]{2,1,0:T(8,128)} custom-call(f32[8,32,64]{2,1,0:T(8,128)} %bitcast.81), custom_call_target="tpu_custom_call" | custom-call | tf_op jit(solution)/shard_map/pallas_call | solution.py:422
  131.3 0.9 slice_divide_fusion
  132.2 0.6 slice_reduce_fusion.1
  132.8 0.6 slice_reduce_fusion
  133.6 0.5 copy-done.7
  134.1 0.1 copy-done.6
  (38 shorter events, 0.3 us)
Async XLA Ops:
  7.2 46.5 %copy-start.4 = (bf16[2,512,128]{2,1,0:T(8,128)(2,1)S(1)}, bf16[2,512,128]{2,1,0:T(8,128)(2,1)}, u32[]{:S(2)}) copy-start(bf16[2,512,128]{2,1,0:T(8,128)(2,1)} %constant.140.clone.pool) | copy-start | bytes 786436
  7.2 81.4 %all-gather.2.cloned.1.call-start = ((), (), s32[]{:S(2)}) async-start(), calls=%async_computation | async-start | bytes 1179648 | tf_op jit(solution)/shard_map/all_gather | solution.py:461
  12.2 1.0 copy-start.3
  13.1 0.8 copy-start.5
  37.0 47.8 %copy-start = (bf16[33,64,512]{2,1,0:T(8,128)(2,1)}, bf16[33,64,512]{2,1,0:T(8,128)(2,1)S(1)}, u32[]{:S(2)}) copy-start(bf16[33,64,512]{2,1,0:T(8,128)(2,1)S(1)} %get-tuple-element.18.table) | copy-start | bytes 6488068
  67.5 1.7 %copy-start.2 = (f32[24,64,512]{2,1,0:T(8,128)}, f32[24,64,512]{2,1,0:T(8,128)S(1)}, u32[]{:S(2)}) copy-start(f32[24,64,512]{2,1,0:T(8,128)S(1)} %get-tuple-element.21.slope) | copy-start | bytes 9437188
  84.9 1.0 copy-start.1
  133.5 0.6 copy-start.7
  133.6 0.6 copy-start.6
Sparse Core Ops, SparseCore 0:
  37.2 40.6 all-gather.1

commit v4 on v3

--- a/solution.py
+++ b/solution.py
@@ -63,12 +63,51 @@
             views[tap * width : (tap + 1) * width, :] = out.astype(BF16)
 
 
-def forward_kernel(near, table, weight, bias, pool, slope, octants, views):
+def place_of(counts):
+    me = lax.axis_index("blocks")
+
+    def add(d, sums):
+        held = counts[d]
+        return sums[0] + jnp.where(d < me, held, 0), sums[1] + held
+
+    first, total = lax.fori_loop(0, counts.shape[0], add, (jnp.int32(0), jnp.int32(0)))
+    return first, counts[me], total
+
+
+def owner_of(counts, block):
+    def step(d, state):
+        owner, start, here = state
+        covers = here <= block
+        return jnp.where(covers, d, owner), jnp.where(covers, here, start), here + counts[d]
+
+    zero = jnp.int32(0)
+    owner, start, _ = lax.fori_loop(0, counts.shape[0], step, (zero, zero, zero))
+    return owner, start
+
+
+def near_rows(block, total, row, absent):
+    px, py = block % 2, block // 2 % 2
+    tests = (
+        (px == 1, -1), (px == 0, 1), (py == 1, -2), (py == 0, 2),
+        (block >= 4, -4), (block + 4 < total, 4),
+    )
+    return [jnp.where(test, row(offset), absent) for test, offset in tests]
+
+
+def forward_kernel(counts, table, weight, bias, pool, slope, octants, views):
     width = table.shape[1]
+    first, live, total = place_of(counts)
+    absent = table.shape[0] - 1
+    slots = absent - 16
+
+    def table_row(r):
+        return jnp.where(r < 8 + live, r, jnp.minimum(r + slots - live, absent - 1))
 
     def row(j, carry):
-        own = table[near[j * 7 + 6]]
-        write_views(views, own, [table[near[j * 7 + n]] for n in range(6)], width)
+        block = jnp.maximum(first - 4 + j, 0)
+        near = near_rows(block, total, lambda offset: table_row(j + 4 + offset), absent)
+        own = table[table_row(j + 4)]
+        write_views(views, own, [table[r] for r in near], width)
         v = jnp.dot(weight[...], views[...], preferred_element_type=F32) + bias[...]
         s = sigmoid(v)
         slope[j] = s * (1.0 + v * (1.0 - s))
@@ -88,14 +127,21 @@
 
 
 def backward_kernel(
-    near, facts, octant_at, cotangent_at, table, slope, octants, cotangent, forward_w, coarse_b, back_coarse_w, back_w,
+    counts, table, slope, octants, cotangent, forward_w, coarse_b, back_coarse_w, back_w,
     place, spread,
     coarse_out, fine_grad, fine_wg, fine_bg, coarse_wg, coarse_bg,
     views, coarse_in, coarse_act, coarse_delta, coarse_back, fine_delta, bias_sum,
 ):
     width = table.shape[1]
     slots, group = fine_grad.shape[0], fine_grad.shape[1]
-    chan, live, parent0, coarse_row, coarse_live = (facts[n] for n in range(5))
+    chan = lax.axis_index("chan")
+    first, live, total = place_of(counts)
+    parent = (first + 4) // 8 - 1
+    parent0 = (first + 4) % 8
+    coarse_first = (first + 7) // 8
+    coarse_live = (first + live + 7) // 8 - coarse_first
+    coarse_row = coarse_first - parent + 1
+    coarse_begin, coarse_end = 2 - parent, total // 8 - parent + 2
     mine = pl.ds(pl.multiple_of(chan * group, group), group)
 
     def own_views():
@@ -105,16 +151,17 @@
         )
 
     def assemble(k, carry):
-        total = jnp.zeros((width, CELLS), F32)
+        cells = jnp.zeros((width, CELLS), F32)
         for q in range(8):
-            at = octant_at[k * 8 + q]
-            owner, slot = at // slots, at % slots
+            block = jnp.clip((parent - 2 + k) * 8 + q, 0, total - 1)
+            owner, start = owner_of(counts, block)
+            slot = block - start
             both = jnp.concatenate(
                 [octants[c, owner, slot // 2] for c in range(octants.shape[0])], axis=0
             )
-            total += jnp.dot(both, place[slot % 2, q], preferred_element_type=F32)
-        inside = jnp.logical_and(k >= facts[5], k < facts[6])
-        coarse_in[k] = jnp.where(inside, total, 0.0).astype(BF16)
+            cells += jnp.dot(both, place[slot % 2, q], preferred_element_type=F32)
+        inside = jnp.logical_and(k >= coarse_begin, k < coarse_end)
+        coarse_in[k] = jnp.where(inside, cells, 0.0).astype(BF16)
         return carry
 
     lax.fori_loop(0, 8, assemble, 0)
@@ -126,8 +173,11 @@
         v = jnp.dot(forward_w[...], views[...], preferred_element_type=F32) + coarse_b[...]
         s = sigmoid(v)
         coarse_act[k] = (v * s).astype(BF16)
-        inside = jnp.logical_and(k + 1 >= facts[5], k + 1 < facts[6])
-        delta = cotangent[cotangent_at[k]].astype(F32) * (s * (1.0 + v * (1.0 - s)))
+        inside = jnp.logical_and(k + 1 >= coarse_begin, k + 1 < coarse_end)
+        safe = jnp.clip(parent - 1 + k, 0, total // 8 - 1)
+        owner, start = owner_of(counts, safe * 8)
+        row = owner * coarse_out.shape[0] + safe - (start + 7) // 8
+        delta = cotangent[row].astype(F32) * (s * (1.0 + v * (1.0 - s)))
         coarse_delta[k] = jnp.where(inside, delta, 0.0).astype(BF16)
         return carry
 
@@ -180,9 +230,8 @@
     def fine_row(r, carry):
         @pl.when(r < live)
         def _():
-            write_views(
-                views, fine_delta[r + 4], [fine_delta[near[r * 6 + n]] for n in range(6)], width
-            )
+            near = near_rows(first + r, total, lambda offset: r + 4 + offset, slope.shape[0])
+            write_views(views, fine_delta[r + 4], [fine_delta[n] for n in near], width)
             fine_grad[r] = jnp.dot(back_w[...], views[...], preferred_element_type=F32).astype(BF16)
             fine_wg[...] += lax.dot_general(
                 own_views(), table[r + 8], (((1,), (1,)), ((), ())), preferred_element_type=F32
@@ -438,17 +487,10 @@
     channels = fine_weight.shape[2]
     device = lax.axis_index("blocks")
     chan = lax.axis_index("chan")
-    order = jnp.arange(block_counts.shape[0])
-    earlier = order[None, :] < order[:, None]
-    starts = jnp.sum(jnp.where(earlier, block_counts[None, :], 0), axis=1)
-    first = starts[device]
     live = block_counts[device]
     total = jnp.sum(block_counts)
     coarse_total = total // 8
-    coarse_first = (first + 7) // 8
-    coarse_count = (first + live + 7) // 8 - coarse_first
-
-    rows = slots + 16
+
     tail = lax.dynamic_slice_in_dim(fine_input, live - 8, 8, 0)
     table, weights, biases, cotangents = gather_start(
         tail,
@@ -463,22 +505,6 @@
 
     spread, pool, place = (jnp.asarray(a, BF16) for a in octant_maps())
     delta_rows = slots + 8
-    ids = first - 4 + jnp.arange(delta_rows, dtype=jnp.int32)
-    px, py = ids % 2, ids // 2 % 2
-    valid = jnp.stack(
-        [px == 1, px == 0, py == 1, py == 0, ids >= 4, ids + 4 < total], axis=1
-    )
-    offsets = jnp.array([-1, 1, -2, 2, -4, 4], jnp.int32)[None, :]
-    spot = jnp.arange(delta_rows, dtype=jnp.int32)[:, None] + offsets
-
-    def table_row(r):
-        return jnp.where(r < 8 + live, r, jnp.minimum(r + slots - live, rows - 1))
-
-    own_row = table_row(jnp.arange(delta_rows, dtype=jnp.int32) + 4)
-    near_fine = jnp.where(valid, table_row(spot + 4), rows)
-    near_fine = jnp.concatenate([near_fine, own_row[:, None]], axis=1).reshape(-1)
-    near_delta = jnp.where(valid, spot, delta_rows)[4 : 4 + slots].reshape(-1)
-
     smem = pl.BlockSpec(memory_space=pltpu.SMEM)
     vmem = pl.BlockSpec(memory_space=pltpu.VMEM)
     slope, octants = pl.pallas_call(
@@ -492,7 +518,7 @@
         scratch_shapes=[pltpu.VMEM((7 * channels, cells), BF16)],
         compiler_params=pltpu.CompilerParams(vmem_limit_bytes=40 * 2**20),
     )(
-        near_fine,
+        block_counts,
         table,
         full_fine.transpose(1, 0, 2).reshape(channels, 7 * channels),
         biases[0][:, None],
@@ -500,35 +526,6 @@
     )
 
     every_octant = share_octants(octants, group)
-    parent = (first - 4) // 8
-
-    def owner_of(block):
-        below = starts[None, :] <= block[:, None]
-        return (
-            jnp.sum(below.astype(jnp.int32), axis=1) - 1,
-            jnp.max(jnp.where(below, starts[None, :], 0), axis=1),
-        )
-
-    octant_ids = (parent - 2) * 8 + jnp.arange(64, dtype=jnp.int32)
-    safe = jnp.clip(octant_ids, 0, total - 1)
-    owner, start = owner_of(safe)
-    octant_at = owner * slots + safe - start
-    coarse_ids = parent - 1 + jnp.arange(6, dtype=jnp.int32)
-    safe = jnp.clip(coarse_ids, 0, coarse_total - 1)
-    owner, start = owner_of(safe * 8)
-    cotangent_at = owner * coarse_slots + safe - (start + 7) // 8
-
-    facts = jnp.stack(
-        [
-            chan,
-            live,
-            first - 4 - parent * 8,
-            coarse_first - parent + 1,
-            coarse_count,
-            2 - parent,
-            coarse_total - parent + 2,
-        ]
-    ).astype(jnp.int32)
     back_coarse = paired(full_coarse).transpose(2, 0, 1).reshape(channels, 7 * channels)
     back_fine = paired(full_fine).transpose(2, 0, 1).reshape(channels, 7 * channels)
     back_fine = lax.dynamic_slice_in_dim(back_fine, chan * group, group, 0)
@@ -542,7 +539,7 @@
             jax.ShapeDtypeStruct((7 * group, channels), F32),
             jax.ShapeDtypeStruct((group, channels), F32),
         ),
-        in_specs=[smem] * 4 + [vmem] * 10,
+        in_specs=[smem] + [vmem] * 10,
         out_specs=(vmem,) * 6,
         scratch_shapes=[
             pltpu.VMEM((7 * channels, cells), BF16),
@@ -555,10 +552,7 @@
         ],
         compiler_params=pltpu.CompilerParams(vmem_limit_bytes=56 * 2**20),
     )(
-        near_delta,
-        facts,
-        octant_at,
-        cotangent_at,
+        block_counts,
         table,
         slope,
         every_octant,

time: 141 us -> 138 us (0.979)
  Pallas kernels: 93.8 us -> 102 us
  other arithmetic: 10.1 us -> 5.23 us
  between operations: 22.3 us -> 18.9 us
  local copies, waits for them, and re-layouts: 14.8 us -> 11.9 us
    pallas_call x1, Pallas kernels: 17.9 us -> 21.3 us  [sum_over_blocks(): pl.pallas_call(sum_kernel, out_shape=jax.ShapeDtypeStruct(shape, F32), in...]
    pallas_call x1, Pallas kernels: 23.3 us -> 25.4 us  [local(): pl.pallas_call(backward_kernel, out_shape=(jax.ShapeDtypeStruct((coarse_s...]
    pallas_call x1, Pallas kernels: 15.6 us -> 17.7 us  [share_octants(): pl.pallas_call(octant_kernel, out_shape=jax.ShapeDtypeStruct((width, n, o...]
    select_n x2 -> x0, other arithmetic: 2.03 us -> none  [the longest x1 1.37 us: local(): near_fine = jnp.where(valid, table_row(spot + 4), rows)]
    unnamed x35 -> x37, local copies, waits for them, and re-layouts: 5.75 us -> 6.39 us
  transfers between devices with their start and end apart: 1 -> 1, of which waited for: 0 -> 0; matrix products, arithmetic and copies ran while one was open for 9% -> 3% of each run, Pallas kernels for 21% -> 23%
where the time goes in v4:
time: 138 us
  Pallas kernels  102 us (74%)
  between operations  18.9 us (14%)
  local copies, waits for them, and re-layouts  11.9 us (9%)
  other arithmetic  5.23 us (4%)
    pallas_call x1, Pallas kernels, local(): pl.pallas_call(backward_kernel, out_shape=(jax.ShapeDtypeStruct((coarse_s...  25.4 us
    pallas_call x1, Pallas kernels, gather_start(): pl.pallas_call(gather_kernel, out_shape=(jax.ShapeDtypeStruct((slots + 17...  23.1 us
    pallas_call x1, Pallas kernels, sum_over_blocks(): pl.pallas_call(sum_kernel, out_shape=jax.ShapeDtypeStruct(shape, F32), in...  21.3 us
    pallas_call x1, Pallas kernels, share_octants(): pl.pallas_call(octant_kernel, out_shape=jax.ShapeDtypeStruct((width, n, o...  17.7 us
    pallas_call x1, Pallas kernels, local(): pl.pallas_call(forward_kernel, out_shape=(jax.ShapeDtypeStruct((delta_row...  14 us
    unnamed x37, local copies, waits for them, and re-layouts  6.39 us
  transfers between devices with their start and end apart: 1, of which 0 were waited for; matrix products, arithmetic and copies ran while one was open for 3% of the time, Pallas kernels for 23%

profile of v4, /device:TPU:0, one launch (start us, length us, event | category | flops | bytes accessed | tf_op | source)
XLA Modules:
  0.0 137.7 jit_solution(9093004592806528410)
XLA Ops:
  7.2 0.0 copy-start.4
  7.2 0.0 all-gather.2.cloned.1.call-start
  7.2 1.3 dynamic_slice.9
  9.8 0.9 constant_dynamic-slice_fusion.1.tail
  10.7 0.8 pad_maximum_fusion.1.weight
  11.5 0.7 pad_maximum_fusion.2.bias
  12.2 0.0 copy-start.3
  12.2 0.9 copy-done.3
  13.1 0.0 copy-start.5
  13.1 0.8 copy-done.5
  13.9 23.1 %shard_map.145 = (bf16[33,64,512]{2,1,0:T(8,128)(2,1)S(1)}, bf16[14,64,64]{2,1,0:T(8,128)(2,1)S(1)}, f32[4,2,16]{2,1,0:T(2,128)S(1)}, bf16[2,64,512]{2,1,0:T(8,128)(2,1)}) custom-call(bf16[8,16,512]{2,1,0:T(8,128)(2,1)S(1)} %constant_dynamic-slice_fusion.1.tail, bf16[16,16,512]{2,1,0:T(8,128)(2,1)S(1)} %copy-done.3, ...), custom_call_target="tpu_custom_call" | custom-call | tf_op jit(solution)/shard_map/pallas_call | solution.py:402
  37.0 0.0 copy-start
  37.0 0.0 all-gather.2.cloned.1.call-update
  37.1 1.3 reduce_sum.9
  41.1 0.1 constant_dynamic-slice_fusion
  41.2 0.7 copy.36.back_w
  41.9 0.7 copy.34.back_coarse_w
  42.6 0.1 copy.28
  42.7 0.1 reshape.59.weight
  42.9 0.1 broadcast_in_dim_squeeze.8.bias
  43.0 0.0 copy-done.4
  43.0 0.0 copy-start.6
  43.0 0.6 copy-done.6
  43.7 14.0 %shard_map.146 = (f32[24,64,512]{2,1,0:T(8,128)S(1)}, bf16[8,64,128]{2,1,0:T(8,128)(2,1)S(1)}) custom-call(s32[8]{0:T(128)S(1)} %copy-done.6, bf16[33,64,512]{2,1,0:T(8,128)(2,1)S(1)} %get-tuple-element.18.table, bf16[64,448]{1,0:T(8,128)(2,1)S(1)} %reshape.59.weight, f32[64,1]{1,0:T(8,128)S(1)} %broadcast_in_dim_squeeze.8.bias, ...), custom_call_target="tpu_custom_call" | custom-call | tf_op jit(solution)/shard_map/pallas_call | solution.py:510
  57.7 0.0 copy-start.2
  57.7 1.6 %copy-done.2 = f32[24,64,512]{2,1,0:T(8,128)} copy-done((f32[24,64,512]{2,1,0:T(8,128)}, f32[24,64,512]{2,1,0:T(8,128)S(1)}, u32[]{:S(2)}) %copy-start.2) | copy-done | bytes 3145752
  59.3 17.7 %shard_map.147.octants = bf16[4,8,8,16,128]{4,3,2,1,0:T(8,128)(2,1)S(1)} custom-call(bf16[8,64,128]{2,1,0:T(8,128)(2,1)S(1)} %get-tuple-element.22.octants), custom_call_target="tpu_custom_call" | custom-call | tf_op jit(solution)/shard_map/pallas_call | solution.py:440
  77.0 0.0 copy-start.1
  77.0 1.0 copy-done.1
  78.0 0.1 copy.30
  78.1 0.8 reshape.60.forward_w
  78.9 0.0 copy-done
  78.9 0.7 broadcast_in_dim_squeeze.9.coarse_b
  80.3 0.0 all-gather.2.cloned.1.call-done.cotangent
  80.4 25.4 %shard_map.148 = (bf16[2,16,512]{2,1,0:T(8,128)(2,1)}, bf16[16,16,512]{2,1,0:T(8,128)(2,1)}, f32[112,64]{1,0:T(8,128)}, f32[16,64]{1,0:T(8,128)}, f32[112,64]{1,0:T(8,128)}, /*index=5*/f32[16,64]{1,0:T(8,128)}) custom-call(s32[8]{0:T(128)} %counts.3, bf16[33,64,512]{2,1,0:T(8,128)(2,1)} %copy-done, f32[24,64,512]{2,1,0:T(8,128)} %copy-done.2, ...), custom_call_target="tpu_custom_call" | custom-call | tf_op jit(solution)/shard_map/pallas_call | solution.py:532
  105.7 1.5 %pad_maximum_fusion = f32[256,64]{1,0:T(8,128)} fusion(f32[16,64]{1,0:T(8,128)} %get-tuple-element.29, f32[112,64]{1,0:T(8,128)} %get-tuple-element.28, f32[16,64]{1,0:T(8,128)} %get-tuple-element.27, f32[112,64]{1,0:T(8,128)} %get-tuple-element.26), kind=kLoop, calls=%fused_computation | loop fusion | flops 49152 | bytes 131072 | tf_op jit(solution)/shard_map/concatenate | solution.py:567
  107.3 21.3 %shard_map.149 = f32[8,32,64]{2,1,0:T(8,128)} custom-call(f32[8,32,64]{2,1,0:T(8,128)} %bitcast.75), custom_call_target="tpu_custom_call" | custom-call | tf_op jit(solution)/shard_map/pallas_call | solution.py:471
  128.6 0.9 slice_divide_fusion
  129.5 0.6 slice_reduce_fusion
  130.2 0.0 copy-start.7
  130.2 0.0 copy-start.8
  130.3 0.6 copy-done.7
  130.9 0.0 copy-done.8
  (22 shorter events, 0.1 us)
Async XLA Ops:
  7.2 35.8 %copy-start.4 = (bf16[2,512,128]{2,1,0:T(8,128)(2,1)S(1)}, bf16[2,512,128]{2,1,0:T(8,128)(2,1)}, u32[]{:S(2)}) copy-start(bf16[2,512,128]{2,1,0:T(8,128)(2,1)} %constant.46.clone.pool) | copy-start | bytes 786436
  7.2 73.2 %all-gather.2.cloned.1.call-start = ((), (), s32[]{:S(2)}) async-start(), calls=%async_computation | async-start | bytes 1179648 | tf_op jit(solution)/shard_map/all_gather | solution.py:503
  12.2 0.9 copy-start.3
  13.1 0.8 copy-start.5
  37.0 41.8 %copy-start = (bf16[33,64,512]{2,1,0:T(8,128)(2,1)}, bf16[33,64,512]{2,1,0:T(8,128)(2,1)S(1)}, u32[]{:S(2)}) copy-start(bf16[33,64,512]{2,1,0:T(8,128)(2,1)S(1)} %get-tuple-element.18.table) | copy-start | bytes 6488068
  43.0 0.7 copy-start.6
  57.7 1.6 %copy-start.2 = (f32[24,64,512]{2,1,0:T(8,128)}, f32[24,64,512]{2,1,0:T(8,128)S(1)}, u32[]{:S(2)}) copy-start(f32[24,64,512]{2,1,0:T(8,128)S(1)} %get-tuple-element.21.slope) | copy-start | bytes 9437188
  77.0 1.0 copy-start.1
  130.2 0.6 copy-start.7
  130.2 0.6 copy-start.8
Sparse Core Ops, SparseCore 0:
  37.2 39.5 all-gather.1
